TPU v7x, 256 devices: a whole 4x4x8 slice. The times are simulated.
256 devices in a mesh: outer: 4 (over x_lo, core), inner: 64 (over z, y, x_hi).
Axes of the slice: x: 4 (x_hi: 2, x_lo: 2; x = x_hi * 2 + x_lo), y: 4, z: 8, core: 2. Of those that a mesh axis runs over, the one named last changes fastest.
Arguments:
- query_rows: bfloat16 [32768, 640], P(('outer', 'inner')), may hold values from -22 to 22
- key_rows: bfloat16 [32768, 128], P(('outer', 'inner')), may hold values from -4.5 to 4.5
- value_rows: bfloat16 [32768, 128], P(('outer', 'inner')), may hold values from -6 to 6
- positions: int32 [32768], P(('outer', 'inner')), may hold values from 0 to 32767, as said below
Outputs:
- attended: bfloat16 [32768, 640], P(('outer', 'inner'))
Inputs may be any that keep to these rules, and one draw needn't show every extreme that they name: positions is a permutation of the sequence's positions; each aligned run of 64 rows holds 64 consecutive positions in rising order.
All inputs are finite; a program needn't handle non-finite values.
Results may differ from a plain program's by a relative error of at most 0.0095.
Values may be sent and summed in bfloat16 or wider, within the bound.
No kernel may reach another device: no remote copies, remote signals or barrier semaphores. Data moves between devices by JAX's collectives and lax.ppermute only.
A program may use at most 128 MiB of HBM per device.

v0:
```python
import functools
import math

import jax
import jax.numpy as jnp
from jax import lax
from jax.experimental import pallas as pl
from jax.experimental.pallas import tpu as pltpu
from jax.sharding import Mesh, PartitionSpec as P

HD = 128
HEADS = 5
HALF = 64
LOCAL = 128
QRUNS = 8
BLOCK_RUNS = 4
BLOCK = BLOCK_RUNS * HALF
COLS = 4 * HALF
SLABS = QRUNS * HEADS * HALF // COLS
ACC_ROWS = HD + 16
GROUP = 8
NOTE = 16
FACTS = 32
SCALE2 = math.log2(math.e) / math.sqrt(HD)
NEVER = -1e30
SHUT = 1e30
SUM_LIMIT = 1e36

AXES = ("xl", "c", "z", "y", "xh")
STATE = (
    jax.ShapeDtypeStruct((QRUNS, HD), jnp.float32),
    jax.ShapeDtypeStruct((SLABS + 1, HD, COLS), jnp.bfloat16),
    jax.ShapeDtypeStruct((SLABS + 1, ACC_ROWS, COLS), jnp.float32),
    jax.ShapeDtypeStruct((SLABS + 1, 1, COLS), jnp.float32),
)


def runs_of_slab(n):
    return [n] * 4 if n < QRUNS else [(n - QRUNS) * 4 + w for w in range(4)]


def head_of_slab(n, w):
    return w if n < QRUNS else HEADS - 1


def attend_kernel(first, ys, n_kv, n_wait, *refs):
    refs = list(refs)
    last = ys is not None
    mine = list(ys) if last else list(range(QRUNS // 2))
    my_runs = [2 * y + r for y in mine for r in range(2)]
    my_slabs = [n for n in range(SLABS) if runs_of_slab(n)[0] in my_runs]

    def take(n):
        got = refs[:n]
        del refs[:n]
        return got

    if first:
        q_refs = take(QRUNS // 2)
    kv_refs = take(n_kv)
    if not first:
        seen_ref, qnum_in, qt, accs_in, ms_in = take(5)
    take(n_wait)
    if last:
        o_refs = take(len(mine))
    else:
        (o_ref,) = take(1)
    if first:
        qnum, qt, accs, ms = take(4)
    elif last:
        accs, ms = take(2)
    else:
        accs, ms = take(2)
    ks, vs, vt, s0, s1, places, qrun, facts_v, facts, ps, item_slab, item_block, facts_sem = refs
    runs = 2 * sum(ref.shape[0] for ref in kv_refs)
    blocks = runs // BLOCK_RUNS

    def numbers(note):
        note = note.astype(jnp.float32)
        return note[0:1] * 16 + note[1:2], note[2:3] * 16 + note[3:4]

    i = 0
    for ref in kv_refs:
        for g in range(ref.shape[0]):
            one, two = numbers(ref[g, 2 * LOCAL :, :])
            places[i : i + 1, :] = one
            places[i + 1 : i + 2, :] = two
            i += 2
    places[runs:, :] = jnp.full((places.shape[0] - runs, HD), 1e6, jnp.float32)
    down = places[...]
    across = jnp.transpose(down)
    if first:
        q_rows = [n for ref in q_refs for n in numbers(ref[LOCAL:, :HD])]
        qnum[...] = jnp.concatenate(q_rows, axis=0)
    else:
        q_rows = [qnum_in[a : a + 1, :] for a in range(QRUNS)]

    def count(holds):
        return jnp.sum(jnp.where(holds, 1.0, 0.0), axis=0, keepdims=True)

    facts_v[...] = jnp.concatenate(
        [count(down < across), across[0:1]]
        + q_rows
        + [count(down < q) for q in q_rows]
        + [count(down <= q) for q in q_rows]
        + [jnp.zeros((FACTS - 2 - 3 * QRUNS, HD), jnp.float32)],
        axis=0,
    ).astype(jnp.int32)
    copy = pltpu.make_async_copy(facts_v, facts, facts_sem)
    copy.start()

    group = lax.broadcasted_iota(jnp.int32, (1, HD), 1) // HALF
    for n in range(SLABS):
        of = runs_of_slab(n)
        halves = [jnp.where(group == 0, q_rows[of[v]], q_rows[of[v + 1]]) for v in (0, 2)]
        qrun[n] = jnp.concatenate(halves, axis=1).astype(jnp.int32)
    qrun[SLABS] = jnp.zeros((1, COLS), jnp.int32)
    inside = lax.rem(lax.broadcasted_iota(jnp.int32, (1, COLS), 1), HALF)

    if first:
        for n in range(SLABS):
            rows = []
            for w, a in enumerate(runs_of_slab(n)):
                h = head_of_slab(n, w)
                rows.append(
                    q_refs[a // 2][(a % 2) * HALF : (a % 2 + 1) * HALF, h * HD : (h + 1) * HD]
                )
            slab = jnp.concatenate(rows, axis=0).astype(jnp.float32)
            qt[n] = jnp.transpose(slab).astype(jnp.bfloat16)
        qt[SLABS] = jnp.zeros((HD, COLS), jnp.bfloat16)

    def load_state():
        if first:
            accs[...] = jnp.zeros_like(accs)
            ms[...] = jnp.full_like(ms, NEVER)
        else:
            for n in my_slabs:
                accs[n] = accs_in[n]
                ms[n] = ms_in[n]
            accs[SLABS] = jnp.zeros((ACC_ROWS, COLS), jnp.float32)
        ms[SLABS] = jnp.zeros((1, COLS), jnp.float32)

    load_state()
    copy.wait()

    class Column:
        def __init__(self, start):
            self.start = start

        def __getitem__(self, a):
            return facts[self.start + a, 0]

    below, upto = Column(2 + QRUNS), Column(2 + 2 * QRUNS)

    i = 0
    for ref in kv_refs:
        for g in range(ref.shape[0]):
            for r in range(2):
                rank = facts[0, i]
                at = pl.ds(pl.multiple_of(rank * HALF, HALF), HALF)
                ks[at, :] = ref[g, r * HALF : (r + 1) * HALF, :]
                vs[at, :] = ref[g, LOCAL + r * HALF : LOCAL + (r + 1) * HALF, :]
                ps[rank] = facts[1, i]
                i += 1
    for b in range(blocks):
        turned = jnp.transpose(vs[b * BLOCK : (b + 1) * BLOCK, :].astype(jnp.float32))
        vt[b, :HD, :] = turned.astype(jnp.bfloat16)
        vt[b, HD:, :] = jnp.ones((ACC_ROWS - HD, BLOCK), jnp.bfloat16)

    down_run = lax.broadcasted_iota(jnp.int32, (HALF, COLS), 0)

    def first_shift():
        for n in my_slabs:
            s = jnp.dot(ks[:HALF, :], qt[n], preferred_element_type=jnp.float32) * SCALE2
            ok = down_run <= (qrun[n] - ps[0]) * HALF + inside
            top = jnp.max(jnp.where(ok, s, NEVER), axis=0, keepdims=True)
            ms[n] = top if first else jnp.where(ms[n] > 0.5 * NEVER, ms[n], top)

    if first:
        first_shift()
    else:
        fewest = functools.reduce(jnp.minimum, [seen_ref[a] for a in my_runs])
        pl.when(fewest == 0)(first_shift)

    count = 0
    for n in my_slabs:

        def add(b, k, n=n):
            item_slab[k] = n
            item_block[k] = b
            return k + 1

        end = functools.reduce(jnp.maximum, [below[a] for a in set(runs_of_slab(n))])
        count = lax.fori_loop(0, pl.cdiv(end, BLOCK_RUNS), add, count)
    for e in range(2 * GROUP):
        item_slab[count + e] = SLABS
        item_block[count + e] = 0

    def score(n, b):
        at = pl.ds(pl.multiple_of(b * BLOCK, BLOCK), BLOCK)
        return jnp.dot(ks[at, :], qt[n], preferred_element_type=jnp.float32)

    def consume(s, k):
        n, b = item_slab[k], item_block[k]
        mine, shift = qrun[n], ms[n]
        parts = []
        for t in range(BLOCK_RUNS):
            low = jnp.where(ps[b * BLOCK_RUNS + t] < mine, shift, SHUT)
            p = jnp.exp2(s[t * HALF : (t + 1) * HALF] * SCALE2 - low)
            parts.append(p.astype(jnp.bfloat16))
        p = jnp.concatenate(parts, axis=0)
        accs[n] += jnp.dot(vt[b], p, preferred_element_type=jnp.float32)

    def phase(now, later, base):
        for g in range(GROUP):
            k = base + GROUP + g
            later[g] = score(item_slab[k], item_block[k])
            consume(now[g], base + g)

    @pl.when(count > 0)
    def _():
        for g in range(GROUP):
            s0[g] = score(item_slab[g], item_block[g])
        phases = pl.cdiv(count, GROUP)

        def two(k, c):
            phase(s0, s1, 2 * GROUP * k)
            phase(s1, s0, 2 * GROUP * k + GROUP)
            return c

        lax.fori_loop(0, phases // 2, two, 0)

        @pl.when(lax.rem(phases, 2) == 1)
        def _():
            for g in range(GROUP):
                consume(s0[g], (phases - 1) * GROUP + g)

    def diagonal(a, c):
        @pl.when(upto[a] > below[a])
        def _():
            at = pl.ds(pl.multiple_of(below[a] * HALF, HALF), HALF)
            for n in (a, QRUNS + a // 4):
                s = jnp.dot(ks[at, :], qt[n], preferred_element_type=jnp.float32)
                ok = jnp.logical_and(qrun[n] == facts[2 + a, 0], down_run <= inside)
                p = jnp.where(ok, jnp.exp2(s * SCALE2 - ms[n]), 0.0).astype(jnp.bfloat16)
                accs[n, :HD, :] += lax.dot_general(
                    vs[at, :], p, (((0,), (0,)), ((), ())), preferred_element_type=jnp.float32
                )
                accs[n, HD:, :] += jnp.sum(p.astype(jnp.float32), axis=0, keepdims=True)

        return c

    lax.fori_loop(my_runs[0], my_runs[-1] + 1, diagonal, 0)

    worst = jnp.zeros((1, COLS), jnp.int32)
    for n in my_slabs:
        worst = jnp.maximum(worst, jnp.where(accs[n, HD : HD + 1, :] < SUM_LIMIT, 0, 1))

    @pl.when(jnp.max(worst) > 0)
    def _():
        load_state()

        def per_slab(n, c):
            def online(b, c):
                s = score(n, b) * SCALE2
                keep = jnp.concatenate(
                    [
                        jnp.where(
                            down_run <= (qrun[n] - ps[b * BLOCK_RUNS + t]) * HALF + inside, 0.0, 1.0
                        )
                        for t in range(BLOCK_RUNS)
                    ],
                    axis=0,
                )
                old = ms[n]
                s = jnp.where(keep > 0, NEVER, s)
                new = jnp.maximum(old, jnp.max(s, axis=0, keepdims=True))
                p = jnp.where(keep > 0, 0.0, jnp.exp2(s - new))
                ms[n] = new
                accs[n] = accs[n] * jnp.exp2(old - new) + jnp.dot(
                    vt[b], p.astype(jnp.bfloat16), preferred_element_type=jnp.float32
                )
                return c

            return lax.fori_loop(0, blocks, online, c)

        for n in my_slabs:
            per_slab(n, 0)

    if not last:
        for a in range(QRUNS):
            o_ref[a] = upto[a] if first else seen_ref[a] + upto[a]
        return
    levels = {}
    for n in my_slabs:
        total = accs[n, HD : HD + 1, :]
        some = total > 0
        safe = jnp.where(some, total, 1.0)
        levels[n] = jnp.where(some, ms[n] + jnp.log2(safe), NEVER)
        out = jnp.transpose(accs[n, :HD, :] / safe).astype(jnp.bfloat16)
        for w, a in enumerate(runs_of_slab(n)):
            h = head_of_slab(n, w)
            o_refs[mine.index(a // 2)][
                (a % 2) * HALF : (a % 2 + 1) * HALF, h * HD : (h + 1) * HD
            ] = out[w * HALF : (w + 1) * HALF]
    low_half = lax.broadcasted_iota(jnp.int32, (8, HD), 1) < HALF

    def piece(n, v):
        return jnp.broadcast_to(levels[n][:, v * HD : (v + 1) * HD], (8, HD))

    for y in mine:
        rows = []
        for h in range(HEADS - 1):
            one, two = piece(2 * y, h // 2), piece(2 * y + 1, h // 2)
            if h % 2:
                one = pltpu.roll(one, HALF, 1)
            else:
                two = pltpu.roll(two, HALF, 1)
            rows.append(jnp.where(low_half, one, two))
        rows.append(piece(QRUNS + y // 2, y % 2))
        level = jnp.concatenate(rows, axis=1)[:1]
        high = level.astype(jnp.bfloat16).astype(jnp.float32)
        middle = (level - high).astype(jnp.bfloat16).astype(jnp.float32)
        low = level - high - middle
        note = jnp.concatenate(
            [high, middle, low, jnp.zeros((NOTE - 3, HEADS * HD), jnp.float32)], axis=0
        )
        o_refs[mine.index(y)][LOCAL:, :] = note.astype(jnp.bfloat16)


def attend(queries, blocks, state, name, ys=None, wait=()):
    first = not state
    last = ys is not None
    runs = 2 * sum(b.shape[0] for b in blocks)
    smem = pl.BlockSpec(memory_space=pltpu.SMEM)
    vmem = pl.BlockSpec(memory_space=pltpu.VMEM)
    items = SLABS * (runs // BLOCK_RUNS) + 2 * GROUP + 8
    scratch = [
        pltpu.VMEM((runs * HALF, HD), jnp.bfloat16),
        pltpu.VMEM((runs * HALF, HD), jnp.bfloat16),
        pltpu.VMEM((runs // BLOCK_RUNS, ACC_ROWS, BLOCK), jnp.bfloat16),
        pltpu.VMEM((GROUP, BLOCK, COLS), jnp.float32),
        pltpu.VMEM((GROUP, BLOCK, COLS), jnp.float32),
        pltpu.VMEM((HD, HD), jnp.float32),
        pltpu.VMEM((SLABS + 1, 1, COLS), jnp.int32),
        pltpu.VMEM((FACTS, HD), jnp.int32),
        pltpu.SMEM((FACTS, HD), jnp.int32),
        pltpu.SMEM((runs,), jnp.int32),
        pltpu.SMEM((items,), jnp.int32),
        pltpu.SMEM((items,), jnp.int32),
        pltpu.SemaphoreType.DMA(()),
    ]
    seen = jax.ShapeDtypeStruct((QRUNS,), jnp.int32)
    if last:
        one = jax.ShapeDtypeStruct((LOCAL + NOTE, HEADS * HD), jnp.bfloat16)
        out_shape = (one,) * len(ys)
        out_specs = (vmem,) * len(ys)
        scratch = [pltpu.VMEM(s.shape, s.dtype) for s in STATE[2:]] + scratch
    else:
        out_shape = (seen,) + (STATE if first else STATE[2:])
        out_specs = (smem,) + (vmem,) * (len(out_shape) - 1)
    pairs = QRUNS * HEADS * HALF * runs * HALF // 2
    got = pl.pallas_call(
        functools.partial(attend_kernel, first, ys, len(blocks), len(wait)),
        out_shape=out_shape,
        in_specs=([vmem] * len(queries) if first else [])
        + [vmem] * len(blocks)
        + ([] if first else [smem] + [vmem] * len(STATE))
        + [pl.BlockSpec(memory_space=pl.ANY)] * len(wait),
        out_specs=out_specs,
        scratch_shapes=scratch,
        compiler_params=pltpu.CompilerParams(vmem_limit_bytes=20 * 1024 * 1024),
        cost_estimate=pl.CostEstimate(
            flops=4 * pairs * HD, bytes_accessed=runs * HALF * HD * 4, transcendentals=pairs
        ),
        name=name,
    )(*(queries if first else []), *blocks, *state, *wait)
    if last:
        return got
    return got if first else (got[0],) + state[1:3] + got[1:]


def combine_kernel(*refs):
    *o_refs, out_ref = refs
    levels = []
    for o_ref in o_refs:
        note = o_ref[LOCAL:, :].astype(jnp.float32)
        row = note[0:1] + note[1:2] + note[2:3]
        heads = [row[:, h * HD : (h + 1) * HD] for h in range(HEADS)]
        levels.append(
            jnp.concatenate(heads + [jnp.zeros((8 - HEADS, HD), jnp.float32)], axis=0)
        )
    top = functools.reduce(jnp.maximum, levels)
    weights = [jnp.exp2(level - top) for level in levels]
    total = functools.reduce(jnp.add, weights)
    columns = [jnp.transpose(w / total) for w in weights]
    for h in range(HEADS):
        at = slice(h * HD, (h + 1) * HD)
        terms = [
            o_ref[:LOCAL, at].astype(jnp.float32) * column[:, h : h + 1]
            for o_ref, column in zip(o_refs, columns)
        ]
        out_ref[:, at] = functools.reduce(jnp.add, terms).astype(jnp.bfloat16)


def combine(parts):
    vmem = pl.BlockSpec(memory_space=pltpu.VMEM)
    return pl.pallas_call(
        combine_kernel,
        out_shape=jax.ShapeDtypeStruct((LOCAL, HEADS * HD), jnp.bfloat16),
        in_specs=[vmem] * len(parts),
        out_specs=vmem,
        compiler_params=pltpu.CompilerParams(vmem_limit_bytes=8 * 1024 * 1024),
        name="combine",
    )(*parts)


def shift(x, axis, n, by):
    return lax.ppermute(x, axis, [(i, (i + by) % n) for i in range(n)])


def after(arrays, tokens):
    arrays, tokens = list(arrays), list(tokens)

    def nothing(*refs):
        del refs

    whole = pl.BlockSpec(memory_space=pl.ANY)
    got = pl.pallas_call(
        nothing,
        out_shape=[jax.ShapeDtypeStruct(x.shape, x.dtype) for x in arrays],
        in_specs=[whole] * (len(tokens) + len(arrays)),
        out_specs=[whole] * len(arrays),
        input_output_aliases={len(tokens) + i: i for i in range(len(arrays))},
        compiler_params=pltpu.CompilerParams(vmem_limit_bytes=1024 * 1024),
        name="after",
    )(*tokens, *arrays)
    return list(got)


def pack_kernel(place_hbm, q_hbm, k_hbm, v_hbm, kv_out, q_out, place_ref, kv_ref, q_ref, sems):
    copies = [
        pltpu.make_async_copy(place_hbm, place_ref, sems.at[0]),
        pltpu.make_async_copy(k_hbm, kv_ref.at[0], sems.at[1]),
        pltpu.make_async_copy(v_hbm, kv_ref.at[1], sems.at[2]),
        pltpu.make_async_copy(q_hbm, q_ref, sems.at[3]),
    ]
    for copy in copies:
        copy.start()
    for copy in copies:
        copy.wait()
    numbers = [lax.div(place_ref[r * HALF], HALF) for r in range(2)]
    digits = [d for n in numbers for d in (lax.div(n, 16), lax.rem(n, 16))]

    def note(width):
        row = lax.broadcasted_iota(jnp.int32, (NOTE, width), 0)
        got = jnp.zeros((NOTE, width), jnp.int32)
        for i, digit in enumerate(digits):
            got = jnp.where(row == i, digit, got)
        return got.astype(jnp.float32).astype(jnp.bfloat16)

    for i in range(kv_out.shape[0]):
        kv_out[i, :LOCAL, :] = kv_ref[0]
        kv_out[i, LOCAL : 2 * LOCAL, :] = kv_ref[1]
        kv_out[i, 2 * LOCAL :, :] = note(HD)
    q_out[:LOCAL, :] = q_ref[...]
    q_out[LOCAL:, :] = note(HEADS * HD)


def pack(positions, queries, keys, values):
    vmem = pl.BlockSpec(memory_space=pltpu.VMEM)
    return pl.pallas_call(
        pack_kernel,
        out_shape=(
            jax.ShapeDtypeStruct((8, 2 * LOCAL + NOTE, HD), jnp.bfloat16),
            jax.ShapeDtypeStruct((LOCAL + NOTE, HEADS * HD), jnp.bfloat16),
        ),
        in_specs=[pl.BlockSpec(memory_space=pl.ANY)] * 4,
        out_specs=(vmem, vmem),
        scratch_shapes=[
            pltpu.SMEM((LOCAL,), jnp.int32),
            pltpu.VMEM((2, LOCAL, HD), jnp.bfloat16),
            pltpu.VMEM((LOCAL, HEADS * HD), jnp.bfloat16),
            pltpu.SemaphoreType.DMA((4,)),
        ],
        compiler_params=pltpu.CompilerParams(vmem_limit_bytes=56 * 1024 * 1024),
        name="pack",
    )(positions, queries, keys, values)


def halves_kernel(up_ref, down_ref, up_out, down_out):
    up_out[...] = up_ref[: up_out.shape[0]]
    down_out[...] = down_ref[down_out.shape[0] :]


def halves(up, down):
    vmem = pl.BlockSpec(memory_space=pltpu.VMEM)
    half = jax.ShapeDtypeStruct((up.shape[0] // 2,) + up.shape[1:], up.dtype)
    return pl.pallas_call(
        halves_kernel,
        out_shape=(half, half),
        in_specs=[vmem, vmem],
        out_specs=(vmem, vmem),
        compiler_params=pltpu.CompilerParams(vmem_limit_bytes=1024 * 1024),
        name="halves",
    )(up, down)


def local(query_rows, key_rows, value_rows, positions):
    kv, qn = pack(positions, query_rows, key_rows, value_rows)

    def swap(blocks):
        return [shift(b, "c", 2, 1) for b in blocks]

    def pass_on(up, down):
        ring = (0, 2, 1, 3)
        step = [(ring[x], ring[(x + 1) % 4]) for x in range(4)]
        back = [(b, a) for a, b in step]
        return [lax.ppermute(up, ("xl", "xh"), step), lax.ppermute(down, ("xl", "xh"), back)]

    own = lax.all_to_all(kv, "z", 0, 0)
    q1, q2, q3 = (shift(qn, "y", 4, k) for k in (1, 2, 3))
    queries = [q1, q3, q2, qn]
    (own,) = after([own], [q1, q2, q3])
    one = pass_on(own, own)
    own_c = swap([own])
    state = attend(queries, [own] + own_c, (), "attend_0")
    one = after(one, [state[0]])
    two = pass_on(*halves(*one))
    one_c = swap(one)
    state = attend(queries, one + one_c, state, "attend_1")
    two = after(two, [state[0]])
    rest = two + swap(two)
    o1, o3 = attend(queries, rest, state, "attend_2", ys=(0, 1))
    r1, r3 = shift(o1, "y", 4, -1), shift(o3, "y", 4, 1)
    o2, o0 = attend(queries, rest, state, "attend_3", ys=(2, 3), wait=[o1])
    (o2,) = after([o2], [r1, r3])
    return combine([o0, r1, shift(o2, "y", 4, -2), r3])


def solution(mesh):
    fine = Mesh(mesh.devices.reshape(2, 2, 8, 4, 2), AXES)
    rows = P(AXES, None)
    return jax.shard_map(
        local, mesh=fine, in_specs=(rows, rows, rows, P(AXES)), out_specs=rows, check_vma=False
    )
```

profile of v0, /device:TPU:6, one launch (start us, length us, event | category | flops | bytes accessed | tf_op | source)
XLA Modules:
  0.0 119.4 jit_solution(15008066433655562606)
XLA Ops:
  0.0 1.9 %pack.1 = (bf16[8,272,128]{2,1,0:T(8,128)(2,1)}, bf16[144,640]{1,0:T(8,128)(2,1)}) custom-call(s32[128]{0:T(128)} %place_hbm.1, bf16[128,640]{1,0:T(8,128)(2,1)} %q_hbm.1, bf16[128,128]{1,0:T(8,128)(2,1)} %k_hbm.1, bf16[128,128]{1,0:T(8,128)(2,1)} %v_hbm.1), custom_call_target="tpu_custom_call" | custom-call | tf_op jit(solution)/shard_map/pack/pallas_call | solution.py:472
  2.0 0.0 copy-start
  2.0 8.6 %all-to-all-start = ((bf16[8,272,128]{2,1,0:T(8,128)(2,1)}), bf16[8,272,128]{2,1,0:T(8,128)(2,1)S(1)}, u32[]{:S(2)}, u32[]{:S(2)}) async-start(bf16[8,272,128]{2,1,0:T(8,128)(2,1)} %get-tuple-element.26), calls=%async_computation | async-start | bytes 1114112 | tf_op jit(solution)/shard_map/all_to_all | solution.py:521
  10.6 1.6 %collective-permute-start = (bf16[144,640]{1,0:T(8,128)(2,1)}, bf16[144,640]{1,0:T(8,128)(2,1)S(1)}, u32[]{:S(2)}, u32[]{:S(2)}) collective-permute-start(bf16[144,640]{1,0:T(8,128)(2,1)} %get-tuple-element.25.refs_3_), channel_id=1, source_target_pairs={{0,2},{2,4},{4,6},{6,0},{1,3},{3,5},{5,7},{7,1},{8,10},{10,12},{12... | collective-permute-start | bytes 552968 | tf_op jit(solution)/shard_map/ppermute | solution.py:419
  12.2 1.7 %collective-permute-start.1 = (bf16[144,640]{1,0:T(8,128)(2,1)}, bf16[144,640]{1,0:T(8,128)(2,1)S(1)}, u32[]{:S(2)}, u32[]{:S(2)}) collective-permute-start(bf16[144,640]{1,0:T(8,128)(2,1)} %get-tuple-element.25.refs_3_), channel_id=1, source_target_pairs={{0,6},{2,0},{4,2},{6,4},{1,7},{3,1},{5,3},{7,5},{8,14},{10,8},{12,... | collective-permute-start | bytes 552968 | tf_op jit(solution)/shard_map/ppermute | solution.py:419
  13.8 2.0 %collective-permute-start.2 = (bf16[144,640]{1,0:T(8,128)(2,1)}, bf16[144,640]{1,0:T(8,128)(2,1)S(1)}, u32[]{:S(2)}, u32[]{:S(2)}) collective-permute-start(bf16[144,640]{1,0:T(8,128)(2,1)} %get-tuple-element.25.refs_3_), channel_id=1, source_target_pairs={{0,4},{2,6},{4,0},{6,2},{1,5},{3,7},{5,1},{7,3},{8,12},{10,14},{12... | collective-permute-start | bytes 552968 | tf_op jit(solution)/shard_map/ppermute | solution.py:419
  15.8 2.6 %collective-permute-done.refs_0_ = bf16[144,640]{1,0:T(8,128)(2,1)S(1)} collective-permute-done((bf16[144,640]{1,0:T(8,128)(2,1)}, bf16[144,640]{1,0:T(8,128)(2,1)S(1)}, u32[]{:S(2)}, u32[]{:S(2)}) %collective-permute-start) | collective-permute-done | bytes 184352 | tf_op jit(solution)/shard_map/ppermute | solution.py:419
  18.4 3.2 %collective-permute-done.1.refs_2_.refs_1_ = bf16[144,640]{1,0:T(8,128)(2,1)S(1)} collective-permute-done((bf16[144,640]{1,0:T(8,128)(2,1)}, bf16[144,640]{1,0:T(8,128)(2,1)S(1)}, u32[]{:S(2)}, u32[]{:S(2)}) %collective-permute-start.1) | collective-permute-done | bytes 184352 | tf_op jit(solution)/shard_map/ppermute | solution.py:419
  21.6 1.7 %collective-permute-done.2.refs_1_.refs_2_ = bf16[144,640]{1,0:T(8,128)(2,1)S(1)} collective-permute-done((bf16[144,640]{1,0:T(8,128)(2,1)}, bf16[144,640]{1,0:T(8,128)(2,1)S(1)}, u32[]{:S(2)}, u32[]{:S(2)}) %collective-permute-start.2) | collective-permute-done | bytes 184352 | tf_op jit(solution)/shard_map/ppermute | solution.py:419
  23.3 5.5 %all-to-all-done.refs_3_ = bf16[8,272,128]{2,1,0:T(8,128)(2,1)S(1)} async-done(((bf16[8,272,128]{2,1,0:T(8,128)(2,1)}), bf16[8,272,128]{2,1,0:T(8,128)(2,1)S(1)}, u32[]{:S(2)}, u32[]{:S(2)}) %all-to-all-start) | async-done | bytes 557088 | tf_op jit(solution)/shard_map/all_to_all | solution.py:521
  28.8 0.0 collective-permute-start.3
  28.8 0.5 collective-permute-start.4
  29.3 1.5 %collective-permute-start.5 = (bf16[8,272,128]{2,1,0:T(8,128)(2,1)S(1)}, bf16[8,272,128]{2,1,0:T(8,128)(2,1)S(1)}, u32[]{:S(2)}, u32[]{:S(2)}) collective-permute-start(bf16[8,272,128]{2,1,0:T(8,128)(2,1)S(1)} %after.4.refs_4_), channel_id=1, source_target_pairs={{128,0},{1,128},{129,1},{0,129},{130,2},{3,130},{131,3},{2,131},{1... | collective-permute-start | bytes 1671176 | tf_op jit(solution)/shard_map/ppermute | solution.py:519
  30.8 0.0 collective-permute-done.3.refs_5_
  30.8 0.0 copy-done
  30.8 43.4 %attend_0.1 = (s32[8]{0:T(128)S(1)}, f32[8,128]{1,0:T(8,128)S(1)}, bf16[11,128,256]{2,1,0:T(8,128)(2,1)S(1)}, f32[11,144,256]{2,1,0:T(8,128)S(1)}, f32[11,1,256]{2,1,0:T(1,128)S(1)}) custom-call(bf16[144,640]{1,0:T(8,128)(2,1)S(1)} %collective-permute-done.refs_0_, bf16[144,640]{1,0:T(8,128)(2,1)S(1)} %collective-permute-done.1.refs_2_.refs_1_, ...), custom_call_target="tpu_custom_call" | custom-call | flops 1342177280 | bytes 1048576 | tf_op jit(solution)/shard_map/attend_0/pallas_call | solution.py:363
  74.3 0.0 collective-permute-done.4.refs_1_
  74.3 0.0 collective-permute-done.5.refs_2_
  74.3 0.8 collective-permute-start.6
  75.1 0.1 collective-permute-start.7
  75.3 0.8 collective-permute-start.8
  76.1 1.3 %collective-permute-start.9 = (bf16[4,272,128]{2,1,0:T(8,128)(2,1)S(1)}, bf16[4,272,128]{2,1,0:T(8,128)(2,1)S(1)}, u32[]{:S(2)}, u32[]{:S(2)}) collective-permute-start(bf16[4,272,128]{2,1,0:T(8,128)(2,1)S(1)} %get-tuple-element.36), channel_id=1, source_target_pairs={{128,0},{1,128},{129,1},{0,129},{130,2},{3,130},{131,3},{2,131},{1... | collective-permute-start | bytes 835592 | tf_op jit(solution)/shard_map/ppermute | solution.py:519
  77.4 0.0 collective-permute-done.6.refs_2_
  77.4 0.1 collective-permute-done.7.refs_3_
  77.5 12.9 %attend_1.1 = (s32[8]{0:T(128)S(1)}, f32[11,144,256]{2,1,0:T(8,128)S(1)}, f32[11,1,256]{2,1,0:T(1,128)S(1)}) custom-call(bf16[8,272,128]{2,1,0:T(8,128)(2,1)S(1)} %get-tuple-element.28.refs_0_.up_ref, bf16[8,272,128]{2,1,0:T(8,128)(2,1)S(1)} %get-tuple-element.29.refs_1_.down_ref, bf16[8,272,128]{2,1,0:T(8,128)(2,1)S(1)} %collective-permute-done.6.refs_2_, ...), custom_call_target="tpu_custom_call" | custom-call | flops 2684354560 | bytes 2097152 | tf_op jit(solution)/shard_map/attend_1/pallas_call | solution.py:363
  90.4 0.0 collective-permute-done.8.refs_1_
  90.4 0.0 collective-permute-done.9.refs_2_
  90.4 1.1 collective-permute-start.10
  91.6 0.1 collective-permute-start.11
  91.7 1.1 collective-permute-done.10.refs_2_
  92.7 0.4 collective-permute-done.11.refs_3_
  93.1 5.4 %attend_2.1 = (bf16[144,640]{1,0:T(8,128)(2,1)S(1)}, bf16[144,640]{1,0:T(8,128)(2,1)S(1)}) custom-call(bf16[4,272,128]{2,1,0:T(8,128)(2,1)S(1)} %get-tuple-element.37.refs_0_, bf16[4,272,128]{2,1,0:T(8,128)(2,1)S(1)} %get-tuple-element.38.refs_1_, bf16[4,272,128]{2,1,0:T(8,128)(2,1)S(1)} %collective-permute-done.10.refs_2_, ...), custom_call_target="tpu_custom_call" | custom-call | flops 1342177280 | bytes 1048576 | tf_op jit(solution)/shard_map/attend_2/pallas_call | solution.py:363
  98.5 3.3 %collective-permute-start.12 = (bf16[144,640]{1,0:T(8,128)(2,1)S(1)}, bf16[144,640]{1,0:T(8,128)(2,1)S(1)}, u32[]{:S(2)}, u32[]{:S(2)}) collective-permute-start(bf16[144,640]{1,0:T(8,128)(2,1)S(1)} %get-tuple-element.41.refs_9_), channel_id=1, source_target_pairs={{0,6},{2,0},{4,2},{6,4},{1,7},{3,1},{5,3},{7,5},{8,14},{10,8},{12,... | collective-permute-start | bytes 552968 | tf_op jit(solution)/shard_map/ppermute | solution.py:419
  101.8 0.0 collective-permute-start.13
  101.8 5.4 %attend_3.1 = (bf16[144,640]{1,0:T(8,128)(2,1)S(1)}, bf16[144,640]{1,0:T(8,128)(2,1)S(1)}) custom-call(bf16[4,272,128]{2,1,0:T(8,128)(2,1)S(1)} %get-tuple-element.37.refs_0_, bf16[4,272,128]{2,1,0:T(8,128)(2,1)S(1)} %get-tuple-element.38.refs_1_, bf16[4,272,128]{2,1,0:T(8,128)(2,1)S(1)} %collective-permute-done.10.refs_2_, ...), custom_call_target="tpu_custom_call" | custom-call | flops 1342177280 | bytes 1048576 | tf_op jit(solution)/shard_map/attend_3/pallas_call | solution.py:363
  107.2 0.0 collective-permute-done.12.refs_0_.refs_1_
  107.2 3.1 %collective-permute-done.13.refs_1_.refs_3_ = bf16[144,640]{1,0:T(8,128)(2,1)S(1)} collective-permute-done((bf16[144,640]{1,0:T(8,128)(2,1)S(1)}, bf16[144,640]{1,0:T(8,128)(2,1)S(1)}, u32[]{:S(2)}, u32[]{:S(2)}) %collective-permute-start.13) | collective-permute-done | bytes 184352 | tf_op jit(solution)/shard_map/ppermute | solution.py:419
  110.2 0.0 collective-permute-start.14
  110.2 7.9 %collective-permute-done.14.refs_2_ = bf16[144,640]{1,0:T(8,128)(2,1)S(1)} collective-permute-done((bf16[144,640]{1,0:T(8,128)(2,1)S(1)}, bf16[144,640]{1,0:T(8,128)(2,1)S(1)}, u32[]{:S(2)}, u32[]{:S(2)}) %collective-permute-start.14) | collective-permute-done | bytes 184352 | tf_op jit(solution)/shard_map/ppermute | solution.py:419
  118.1 1.3 %combine.1 = bf16[128,640]{1,0:T(8,128)(2,1)} custom-call(bf16[144,640]{1,0:T(8,128)(2,1)S(1)} %get-tuple-element.42.refs_0_, bf16[144,640]{1,0:T(8,128)(2,1)S(1)} %collective-permute-done.12.refs_0_.refs_1_, bf16[144,640]{1,0:T(8,128)(2,1)S(1)} %collective-permute-done.14.refs_2_, bf16[144,640]{1,0:T(8,128)(2,1)S(1)} %collective-permute-done.13.refs_1_.refs_3_), custom_call_target="tpu_custom_call" | custom-call | tf_op jit(solution)/shard_map/combine/pallas_call | solution.py:408
  (5 shorter events, 0.0 us)
Async XLA Ops:
  2.0 28.9 %copy-start = (bf16[144,640]{1,0:T(8,128)(2,1)S(1)}, bf16[144,640]{1,0:T(8,128)(2,1)}, u32[]{:S(2)}) copy-start(bf16[144,640]{1,0:T(8,128)(2,1)} %get-tuple-element.25.refs_3_) | copy-start | bytes 552964
  2.0 26.8 %all-to-all-start = ((bf16[8,272,128]{2,1,0:T(8,128)(2,1)}), bf16[8,272,128]{2,1,0:T(8,128)(2,1)S(1)}, u32[]{:S(2)}, u32[]{:S(2)}) async-start(bf16[8,272,128]{2,1,0:T(8,128)(2,1)} %get-tuple-element.26), calls=%async_computation | async-start | bytes 1114112 | tf_op jit(solution)/shard_map/all_to_all | solution.py:521
  10.6 7.9 %collective-permute-start = (bf16[144,640]{1,0:T(8,128)(2,1)}, bf16[144,640]{1,0:T(8,128)(2,1)S(1)}, u32[]{:S(2)}, u32[]{:S(2)}) collective-permute-start(bf16[144,640]{1,0:T(8,128)(2,1)} %get-tuple-element.25.refs_3_), channel_id=1, source_target_pairs={{0,2},{2,4},{4,6},{6,0},{1,3},{3,5},{5,7},{7,1},{8,10},{10,12},{12... | collective-permute-start | bytes 552968 | tf_op jit(solution)/shard_map/ppermute | solution.py:419
  12.2 9.4 %collective-permute-start.1 = (bf16[144,640]{1,0:T(8,128)(2,1)}, bf16[144,640]{1,0:T(8,128)(2,1)S(1)}, u32[]{:S(2)}, u32[]{:S(2)}) collective-permute-start(bf16[144,640]{1,0:T(8,128)(2,1)} %get-tuple-element.25.refs_3_), channel_id=1, source_target_pairs={{0,6},{2,0},{4,2},{6,4},{1,7},{3,1},{5,3},{7,5},{8,14},{10,8},{12,... | collective-permute-start | bytes 552968 | tf_op jit(solution)/shard_map/ppermute | solution.py:419
  13.8 9.5 %collective-permute-start.2 = (bf16[144,640]{1,0:T(8,128)(2,1)}, bf16[144,640]{1,0:T(8,128)(2,1)S(1)}, u32[]{:S(2)}, u32[]{:S(2)}) collective-permute-start(bf16[144,640]{1,0:T(8,128)(2,1)} %get-tuple-element.25.refs_3_), channel_id=1, source_target_pairs={{0,4},{2,6},{4,0},{6,2},{1,5},{3,7},{5,1},{7,3},{8,12},{10,14},{12... | collective-permute-start | bytes 552968 | tf_op jit(solution)/shard_map/ppermute | solution.py:419
  28.8 2.0 %collective-permute-start.3 = (bf16[8,272,128]{2,1,0:T(8,128)(2,1)S(1)}, bf16[8,272,128]{2,1,0:T(8,128)(2,1)S(1)}, u32[]{:S(2)}, u32[]{:S(2)}) collective-permute-start(bf16[8,272,128]{2,1,0:T(8,128)(2,1)S(1)} %after.4.refs_4_), channel_id=1, source_target_pairs={{0,64},{64,0},{1,65},{65,1},{2,66},{66,2},{3,67},{67,3},{4,68},{68... | collective-permute-start | bytes 1671176 | tf_op jit(solution)/shard_map/ppermute | solution.py:419
  28.8 45.5 %collective-permute-start.4 = (bf16[8,272,128]{2,1,0:T(8,128)(2,1)S(1)}, bf16[8,272,128]{2,1,0:T(8,128)(2,1)S(1)}, u32[]{:S(2)}, u32[]{:S(2)}) collective-permute-start(bf16[8,272,128]{2,1,0:T(8,128)(2,1)S(1)} %after.4.refs_4_), channel_id=1, source_target_pairs={{0,128},{128,1},{1,129},{129,0},{2,130},{130,3},{3,131},{131,2},{4... | collective-permute-start | bytes 1671176 | tf_op jit(solution)/shard_map/ppermute | solution.py:519
  29.3 45.0 %collective-permute-start.5 = (bf16[8,272,128]{2,1,0:T(8,128)(2,1)S(1)}, bf16[8,272,128]{2,1,0:T(8,128)(2,1)S(1)}, u32[]{:S(2)}, u32[]{:S(2)}) collective-permute-start(bf16[8,272,128]{2,1,0:T(8,128)(2,1)S(1)} %after.4.refs_4_), channel_id=1, source_target_pairs={{128,0},{1,128},{129,1},{0,129},{130,2},{3,130},{131,3},{2,131},{1... | collective-permute-start | bytes 1671176 | tf_op jit(solution)/shard_map/ppermute | solution.py:519
  74.3 3.1 %collective-permute-start.6 = (bf16[8,272,128]{2,1,0:T(8,128)(2,1)S(1)}, bf16[8,272,128]{2,1,0:T(8,128)(2,1)S(1)}, u32[]{:S(2)}, u32[]{:S(2)}) collective-permute-start(bf16[8,272,128]{2,1,0:T(8,128)(2,1)S(1)} %get-tuple-element.28.refs_0_.up_ref), channel_id=1, source_target_pairs={{0,64},{64,0},{1,65},{65,1},{2,66},{66,2},{3,67},{67,3},{4,68},{68... | collective-permute-start | bytes 1671176 | tf_op jit(solution)/shard_map/ppermute | solution.py:419
  75.1 2.4 %collective-permute-start.7 = (bf16[8,272,128]{2,1,0:T(8,128)(2,1)S(1)}, bf16[8,272,128]{2,1,0:T(8,128)(2,1)S(1)}, u32[]{:S(2)}, u32[]{:S(2)}) collective-permute-start(bf16[8,272,128]{2,1,0:T(8,128)(2,1)S(1)} %get-tuple-element.29.refs_1_.down_ref), channel_id=1, source_target_pairs={{0,64},{64,0},{1,65},{65,1},{2,66},{66,2},{3,67},{67,3},{4,68},{68... | collective-permute-start | bytes 1671176 | tf_op jit(solution)/shard_map/ppermute | solution.py:419
  75.3 15.1 %collective-permute-start.8 = (bf16[4,272,128]{2,1,0:T(8,128)(2,1)S(1)}, bf16[4,272,128]{2,1,0:T(8,128)(2,1)S(1)}, u32[]{:S(2)}, u32[]{:S(2)}) collective-permute-start(bf16[4,272,128]{2,1,0:T(8,128)(2,1)S(1)} %get-tuple-element.35), channel_id=1, source_target_pairs={{0,128},{128,1},{1,129},{129,0},{2,130},{130,3},{3,131},{131,2},{4... | collective-permute-start | bytes 835592 | tf_op jit(solution)/shard_map/ppermute | solution.py:519
  76.1 14.3 %collective-permute-start.9 = (bf16[4,272,128]{2,1,0:T(8,128)(2,1)S(1)}, bf16[4,272,128]{2,1,0:T(8,128)(2,1)S(1)}, u32[]{:S(2)}, u32[]{:S(2)}) collective-permute-start(bf16[4,272,128]{2,1,0:T(8,128)(2,1)S(1)} %get-tuple-element.36), channel_id=1, source_target_pairs={{128,0},{1,128},{129,1},{0,129},{130,2},{3,130},{131,3},{2,131},{1... | collective-permute-start | bytes 835592 | tf_op jit(solution)/shard_map/ppermute | solution.py:519
  90.4 2.3 %collective-permute-start.10 = (bf16[4,272,128]{2,1,0:T(8,128)(2,1)S(1)}, bf16[4,272,128]{2,1,0:T(8,128)(2,1)S(1)}, u32[]{:S(2)}, u32[]{:S(2)}) collective-permute-start(bf16[4,272,128]{2,1,0:T(8,128)(2,1)S(1)} %get-tuple-element.37.refs_0_), channel_id=1, source_target_pairs={{0,64},{64,0},{1,65},{65,1},{2,66},{66,2},{3,67},{67,3},{4,68},{68... | collective-permute-start | bytes 835592 | tf_op jit(solution)/shard_map/ppermute | solution.py:419
  91.6 1.6 %collective-permute-start.11 = (bf16[4,272,128]{2,1,0:T(8,128)(2,1)S(1)}, bf16[4,272,128]{2,1,0:T(8,128)(2,1)S(1)}, u32[]{:S(2)}, u32[]{:S(2)}) collective-permute-start(bf16[4,272,128]{2,1,0:T(8,128)(2,1)S(1)} %get-tuple-element.38.refs_1_), channel_id=1, source_target_pairs={{0,64},{64,0},{1,65},{65,1},{2,66},{66,2},{3,67},{67,3},{4,68},{68... | collective-permute-start | bytes 835592 | tf_op jit(solution)/shard_map/ppermute | solution.py:419
  98.5 8.6 %collective-permute-start.12 = (bf16[144,640]{1,0:T(8,128)(2,1)S(1)}, bf16[144,640]{1,0:T(8,128)(2,1)S(1)}, u32[]{:S(2)}, u32[]{:S(2)}) collective-permute-start(bf16[144,640]{1,0:T(8,128)(2,1)S(1)} %get-tuple-element.41.refs_9_), channel_id=1, source_target_pairs={{0,6},{2,0},{4,2},{6,4},{1,7},{3,1},{5,3},{7,5},{8,14},{10,8},{12,... | collective-permute-start | bytes 552968 | tf_op jit(solution)/shard_map/ppermute | solution.py:419
  101.8 8.5 %collective-permute-start.13 = (bf16[144,640]{1,0:T(8,128)(2,1)S(1)}, bf16[144,640]{1,0:T(8,128)(2,1)S(1)}, u32[]{:S(2)}, u32[]{:S(2)}) collective-permute-start(bf16[144,640]{1,0:T(8,128)(2,1)S(1)} %get-tuple-element.43), channel_id=1, source_target_pairs={{0,2},{2,4},{4,6},{6,0},{1,3},{3,5},{5,7},{7,1},{8,10},{10,12},{12... | collective-permute-start | bytes 552968 | tf_op jit(solution)/shard_map/ppermute | solution.py:419
  110.2 7.9 %collective-permute-start.14 = (bf16[144,640]{1,0:T(8,128)(2,1)S(1)}, bf16[144,640]{1,0:T(8,128)(2,1)S(1)}, u32[]{:S(2)}, u32[]{:S(2)}) collective-permute-start(bf16[144,640]{1,0:T(8,128)(2,1)S(1)} %after.7), channel_id=1, source_target_pairs={{0,4},{2,6},{4,0},{6,2},{1,5},{3,7},{5,1},{7,3},{8,12},{10,14},{12... | collective-permute-start | bytes 552968 | tf_op jit(solution)/shard_map/ppermute | solution.py:419
where the time goes:
time: 120 us; the launch traced here: 119 us
  Pallas kernels  70.3 us (59%)
  waiting for transfers between devices  25.6 us (21%)
  starting transfers between devices  23.4 us (20%)
    pallas_call x4, Pallas kernels, attend(): pl.pallas_call(functools.partial(attend_kernel, first, ys, len(blocks), l...  67.1 us
    ppermute x11, waiting for transfers between devices, shift(): return lax.ppermute(x, axis, [(i, (i + by) % n) for i in range(n)])  20.1 us
    ppermute x11, starting transfers between devices, shift(): return lax.ppermute(x, axis, [(i, (i + by) % n) for i in range(n)])  10.7 us
    all_to_all x1, starting transfers between devices, local(): own = lax.all_to_all(kv, 'z', 0, 0)  8.61 us
    all_to_all x1, waiting for transfers between devices, local(): own = lax.all_to_all(kv, 'z', 0, 0)  5.49 us
    ppermute x2, starting transfers between devices, pass_on(): lax.ppermute(down, ('xl', 'xh'), back)  2.83 us
  transfers between devices with their start and end apart: 16, of which 9 were waited for; matrix products, arithmetic and copies ran while one was open for 0% of the time, Pallas kernels for 52%

commit v1 on v0

--- a/solution.py
+++ b/solution.py
@@ -48,7 +48,7 @@
     last = ys is not None
     mine = list(ys) if last else list(range(QRUNS // 2))
     my_runs = [2 * y + r for y in mine for r in range(2)]
-    my_slabs = [n for n in range(SLABS) if runs_of_slab(n)[0] in my_runs]
+    my_slabs = [n for n in range(SLABS) if set(runs_of_slab(n)) & set(my_runs)]
 
     def take(n):
         got = refs[:n]
@@ -179,7 +179,7 @@
     if first:
         first_shift()
     else:
-        fewest = functools.reduce(jnp.minimum, [seen_ref[a] for a in my_runs])
+        fewest = functools.reduce(jnp.minimum, [seen_ref[a] for a in range(QRUNS)])
         pl.when(fewest == 0)(first_shift)
 
     count = 0
@@ -299,6 +299,8 @@
         levels[n] = jnp.where(some, ms[n] + jnp.log2(safe), NEVER)
         out = jnp.transpose(accs[n, :HD, :] / safe).astype(jnp.bfloat16)
         for w, a in enumerate(runs_of_slab(n)):
+            if a not in my_runs:
+                continue
             h = head_of_slab(n, w)
             o_refs[mine.index(a // 2)][
                 (a % 2) * HALF : (a % 2 + 1) * HALF, h * HD : (h + 1) * HD
@@ -488,22 +490,27 @@
     )(positions, queries, keys, values)
 
 
-def halves_kernel(up_ref, down_ref, up_out, down_out):
-    up_out[...] = up_ref[: up_out.shape[0]]
-    down_out[...] = down_ref[down_out.shape[0] :]
-
-
-def halves(up, down):
+def pick_kernel(plan, n_in, *refs):
+    for pieces, out_ref in zip(plan, refs[n_in:]):
+        at = 0
+        for source, low, high in pieces:
+            out_ref[at : at + high - low] = refs[source][low:high]
+            at += high - low
+
+
+def pick(arrays, plan):
     vmem = pl.BlockSpec(memory_space=pltpu.VMEM)
-    half = jax.ShapeDtypeStruct((up.shape[0] // 2,) + up.shape[1:], up.dtype)
+    rows = [sum(high - low for _, low, high in pieces) for pieces in plan]
     return pl.pallas_call(
-        halves_kernel,
-        out_shape=(half, half),
-        in_specs=[vmem, vmem],
-        out_specs=(vmem, vmem),
+        functools.partial(pick_kernel, plan, len(arrays)),
+        out_shape=[
+            jax.ShapeDtypeStruct((n,) + arrays[0].shape[1:], arrays[0].dtype) for n in rows
+        ],
+        in_specs=[vmem] * len(arrays),
+        out_specs=[vmem] * len(plan),
         compiler_params=pltpu.CompilerParams(vmem_limit_bytes=1024 * 1024),
-        name="halves",
-    )(up, down)
+        name="pick",
+    )(*arrays)
 
 
 def local(query_rows, key_rows, value_rows, positions):
@@ -520,22 +527,20 @@
 
     own = lax.all_to_all(kv, "z", 0, 0)
     q1, q2, q3 = (shift(qn, "y", 4, k) for k in (1, 2, 3))
-    queries = [q1, q3, q2, qn]
+    queries = [q1, q2, q3, qn]
     (own,) = after([own], [q1, q2, q3])
-    one = pass_on(own, own)
+    one = pass_on(*pick([own], [[(0, 0, 6)], [(0, 2, 8)]]))
     own_c = swap([own])
     state = attend(queries, [own] + own_c, (), "attend_0")
     one = after(one, [state[0]])
-    two = pass_on(*halves(*one))
+    two = pass_on(*pick([own, *one], [[(0, 6, 8), (1, 0, 4)], [(0, 0, 2), (2, 2, 6)]]))
     one_c = swap(one)
     state = attend(queries, one + one_c, state, "attend_1")
     two = after(two, [state[0]])
     rest = two + swap(two)
-    o1, o3 = attend(queries, rest, state, "attend_2", ys=(0, 1))
-    r1, r3 = shift(o1, "y", 4, -1), shift(o3, "y", 4, 1)
-    o2, o0 = attend(queries, rest, state, "attend_3", ys=(2, 3), wait=[o1])
-    (o2,) = after([o2], [r1, r3])
-    return combine([o0, r1, shift(o2, "y", 4, -2), r3])
+    outs = attend(queries, rest, state, "attend_2", ys=(0, 1, 2))
+    (mine,) = attend(queries, rest, state, "attend_3", ys=(3,), wait=outs[:1])
+    return combine([mine] + [shift(o, "y", 4, -k) for k, o in zip((1, 2, 3), outs)])
 
 
 def solution(mesh):

time: 120 us -> 117 us (0.975)
  waiting for transfers between devices: 25.6 us -> 20.7 us
  starting transfers between devices: 23.4 us -> 24.7 us
    ppermute x11, waiting for transfers between devices: 20.1 us -> 13.2 us  [shift(): return lax.ppermute(x, axis, [(i, (i + by) % n) for i in range(n)])]
    ppermute x2, waiting for transfers between devices: 0.01 us -> 2.01 us  [pass_on(): lax.ppermute(down, ('xl', 'xh'), back)]
  transfers between devices with their start and end apart: 16 -> 16, of which waited for: 9 -> 9; matrix products, arithmetic and copies ran while one was open for 0% -> 0% of each run, Pallas kernels for 52% -> 50%
where the time goes in v1:
time: 117 us
  Pallas kernels  71.4 us (61%)
  starting transfers between devices  24.7 us (21%)
  waiting for transfers between devices  20.7 us (18%)
    pallas_call x4, Pallas kernels, attend(): pl.pallas_call(functools.partial(attend_kernel, first, ys, len(blocks), l...  68.1 us
    ppermute x11, waiting for transfers between devices, shift(): return lax.ppermute(x, axis, [(i, (i + by) % n) for i in range(n)])  13.2 us
    ppermute x11, starting transfers between devices, shift(): return lax.ppermute(x, axis, [(i, (i + by) % n) for i in range(n)])  11.7 us
    all_to_all x1, starting transfers between devices, local(): own = lax.all_to_all(kv, 'z', 0, 0)  8.61 us
    all_to_all x1, waiting for transfers between devices, local(): own = lax.all_to_all(kv, 'z', 0, 0)  5.48 us
    ppermute x2, starting transfers between devices, pass_on(): lax.ppermute(down, ('xl', 'xh'), back)  2.37 us
  transfers between devices with their start and end apart: 16, of which 9 were waited for; matrix products, arithmetic and copies ran while one was open for 0% of the time, Pallas kernels for 50%

profile of v1, /device:TPU:6, one launch (start us, length us, event | category | flops | bytes accessed | tf_op | source)
XLA Modules:
  0.0 117.0 jit_solution(8101336222629793260)
XLA Ops:
  0.0 1.9 %pack.1 = (bf16[8,272,128]{2,1,0:T(8,128)(2,1)}, bf16[144,640]{1,0:T(8,128)(2,1)}) custom-call(s32[128]{0:T(128)} %place_hbm.1, bf16[128,640]{1,0:T(8,128)(2,1)} %q_hbm.1, bf16[128,128]{1,0:T(8,128)(2,1)} %k_hbm.1, bf16[128,128]{1,0:T(8,128)(2,1)} %v_hbm.1), custom_call_target="tpu_custom_call" | custom-call | tf_op jit(solution)/shard_map/pack/pallas_call | solution.py:474
  2.0 0.0 copy-start
  2.0 8.6 %all-to-all-start = ((bf16[8,272,128]{2,1,0:T(8,128)(2,1)}), bf16[8,272,128]{2,1,0:T(8,128)(2,1)S(1)}, u32[]{:S(2)}, u32[]{:S(2)}) async-start(bf16[8,272,128]{2,1,0:T(8,128)(2,1)} %get-tuple-element.27), calls=%async_computation | async-start | bytes 1114112 | tf_op jit(solution)/shard_map/all_to_all | solution.py:528
  10.6 1.6 %collective-permute-start = (bf16[144,640]{1,0:T(8,128)(2,1)}, bf16[144,640]{1,0:T(8,128)(2,1)S(1)}, u32[]{:S(2)}, u32[]{:S(2)}) collective-permute-start(bf16[144,640]{1,0:T(8,128)(2,1)} %get-tuple-element.26.refs_3_), channel_id=1, source_target_pairs={{0,2},{2,4},{4,6},{6,0},{1,3},{3,5},{5,7},{7,1},{8,10},{10,12},{12... | collective-permute-start | bytes 552968 | tf_op jit(solution)/shard_map/ppermute | solution.py:421
  12.2 2.9 %collective-permute-start.1 = (bf16[144,640]{1,0:T(8,128)(2,1)}, bf16[144,640]{1,0:T(8,128)(2,1)S(1)}, u32[]{:S(2)}, u32[]{:S(2)}) collective-permute-start(bf16[144,640]{1,0:T(8,128)(2,1)} %get-tuple-element.26.refs_3_), channel_id=1, source_target_pairs={{0,4},{2,6},{4,0},{6,2},{1,5},{3,7},{5,1},{7,3},{8,12},{10,14},{12... | collective-permute-start | bytes 552968 | tf_op jit(solution)/shard_map/ppermute | solution.py:421
  15.1 1.3 %collective-permute-start.2 = (bf16[144,640]{1,0:T(8,128)(2,1)}, bf16[144,640]{1,0:T(8,128)(2,1)S(1)}, u32[]{:S(2)}, u32[]{:S(2)}) collective-permute-start(bf16[144,640]{1,0:T(8,128)(2,1)} %get-tuple-element.26.refs_3_), channel_id=1, source_target_pairs={{0,6},{2,0},{4,2},{6,4},{1,7},{3,1},{5,3},{7,5},{8,14},{10,8},{12,... | collective-permute-start | bytes 552968 | tf_op jit(solution)/shard_map/ppermute | solution.py:421
  16.4 2.0 %collective-permute-done.refs_0_ = bf16[144,640]{1,0:T(8,128)(2,1)S(1)} collective-permute-done((bf16[144,640]{1,0:T(8,128)(2,1)}, bf16[144,640]{1,0:T(8,128)(2,1)S(1)}, u32[]{:S(2)}, u32[]{:S(2)}) %collective-permute-start) | collective-permute-done | bytes 184352 | tf_op jit(solution)/shard_map/ppermute | solution.py:421
  18.4 4.8 %collective-permute-done.1.refs_1_ = bf16[144,640]{1,0:T(8,128)(2,1)S(1)} collective-permute-done((bf16[144,640]{1,0:T(8,128)(2,1)}, bf16[144,640]{1,0:T(8,128)(2,1)S(1)}, u32[]{:S(2)}, u32[]{:S(2)}) %collective-permute-start.1) | collective-permute-done | bytes 184352 | tf_op jit(solution)/shard_map/ppermute | solution.py:421
  23.3 0.0 collective-permute-done.2.refs_2_
  23.3 5.5 %all-to-all-done.refs_3_ = bf16[8,272,128]{2,1,0:T(8,128)(2,1)S(1)} async-done(((bf16[8,272,128]{2,1,0:T(8,128)(2,1)}), bf16[8,272,128]{2,1,0:T(8,128)(2,1)S(1)}, u32[]{:S(2)}, u32[]{:S(2)}) %all-to-all-start) | async-done | bytes 557088 | tf_op jit(solution)/shard_map/all_to_all | solution.py:528
  28.8 0.0 collective-permute-start.3
  28.8 0.1 pick.2
  28.9 0.6 collective-permute-start.4
  29.4 1.5 %collective-permute-start.5 = (bf16[6,272,128]{2,1,0:T(8,128)(2,1)S(1)}, bf16[6,272,128]{2,1,0:T(8,128)(2,1)S(1)}, u32[]{:S(2)}, u32[]{:S(2)}) collective-permute-start(bf16[6,272,128]{2,1,0:T(8,128)(2,1)S(1)} %get-tuple-element.30), channel_id=1, source_target_pairs={{128,0},{1,128},{129,1},{0,129},{130,2},{3,130},{131,3},{2,131},{1... | collective-permute-start | bytes 1253384 | tf_op jit(solution)/shard_map/ppermute | solution.py:526
  31.0 0.0 collective-permute-done.3.refs_5_
  31.0 0.0 copy-done
  31.0 43.4 %attend_0.1 = (s32[8]{0:T(128)S(1)}, f32[8,128]{1,0:T(8,128)S(1)}, bf16[11,128,256]{2,1,0:T(8,128)(2,1)S(1)}, f32[11,144,256]{2,1,0:T(8,128)S(1)}, f32[11,1,256]{2,1,0:T(1,128)S(1)}) custom-call(bf16[144,640]{1,0:T(8,128)(2,1)S(1)} %collective-permute-done.refs_0_, bf16[144,640]{1,0:T(8,128)(2,1)S(1)} %collective-permute-done.1.refs_1_, ...), custom_call_target="tpu_custom_call" | custom-call | flops 1342177280 | bytes 1048576 | tf_op jit(solution)/shard_map/attend_0/pallas_call | solution.py:365
  74.4 0.0 collective-permute-done.4.refs_1_
  74.4 0.0 collective-permute-done.5.refs_2_
  74.5 0.1 collective-permute-start.6
  74.6 0.5 collective-permute-start.7
  75.1 0.1 pick.3
  75.1 1.5 %collective-permute-start.8 = (bf16[6,272,128]{2,1,0:T(8,128)(2,1)S(1)}, bf16[6,272,128]{2,1,0:T(8,128)(2,1)S(1)}, u32[]{:S(2)}, u32[]{:S(2)}) collective-permute-start(bf16[6,272,128]{2,1,0:T(8,128)(2,1)S(1)} %get-tuple-element.38), channel_id=1, source_target_pairs={{0,128},{128,1},{1,129},{129,0},{2,130},{130,3},{3,131},{131,2},{4... | collective-permute-start | bytes 1253384 | tf_op jit(solution)/shard_map/ppermute | solution.py:526
  76.6 0.8 collective-permute-start.9
  77.4 0.0 collective-permute-done.6.refs_2_
  77.4 0.0 collective-permute-done.7.refs_3_
  77.4 10.1 %attend_1.1 = (s32[8]{0:T(128)S(1)}, f32[11,144,256]{2,1,0:T(8,128)S(1)}, f32[11,1,256]{2,1,0:T(1,128)S(1)}) custom-call(bf16[6,272,128]{2,1,0:T(8,128)(2,1)S(1)} %get-tuple-element.31.refs_0_.refs_1_, bf16[6,272,128]{2,1,0:T(8,128)(2,1)S(1)} %get-tuple-element.32.refs_1_.refs_2_, bf16[6,272,128]{2,1,0:T(8,128)(2,1)S(1)} %collective-permute-done.6.refs_2_, ...), custom_call_target="tpu_custom_call" | custom-call | flops 2013265920 | bytes 1572864 | tf_op jit(solution)/shard_map/attend_1/pallas_call | solution.py:365
  87.5 0.0 collective-permute-done.8.refs_1_
  87.5 2.0 %collective-permute-done.9.refs_2_ = bf16[6,272,128]{2,1,0:T(8,128)(2,1)S(1)} collective-permute-done((bf16[6,272,128]{2,1,0:T(8,128)(2,1)S(1)}, bf16[6,272,128]{2,1,0:T(8,128)(2,1)S(1)}, u32[]{:S(2)}, u32[]{:S(2)}) %collective-permute-start.9) | collective-permute-done | bytes 417824 | tf_op jit(solution)/shard_map/ppermute | solution.py:526
  89.5 0.0 collective-permute-start.10
  89.5 0.5 collective-permute-start.11
  90.0 1.2 %collective-permute-done.10.refs_2_ = bf16[6,272,128]{2,1,0:T(8,128)(2,1)S(1)} collective-permute-done((bf16[6,272,128]{2,1,0:T(8,128)(2,1)S(1)}, bf16[6,272,128]{2,1,0:T(8,128)(2,1)S(1)}, u32[]{:S(2)}, u32[]{:S(2)}) %collective-permute-start.10) | collective-permute-done | bytes 417824 | tf_op jit(solution)/shard_map/ppermute | solution.py:421
  91.2 0.6 collective-permute-done.11.refs_3_
  91.8 9.2 %attend_2.1 = (bf16[144,640]{1,0:T(8,128)(2,1)S(1)}, bf16[144,640]{1,0:T(8,128)(2,1)S(1)}, bf16[144,640]{1,0:T(8,128)(2,1)S(1)}) custom-call(bf16[6,272,128]{2,1,0:T(8,128)(2,1)S(1)} %get-tuple-element.40.refs_0_, bf16[6,272,128]{2,1,0:T(8,128)(2,1)S(1)} %get-tuple-element.41.refs_1_, bf16[6,272,128]{2,1,0:T(8,128)(2,1)S(1)} %collective-permute-done.10.refs_2_, ...), custom_call_target="tpu_custom_call" | custom-call | flops 2013265920 | bytes 1572864 | tf_op jit(solution)/shard_map/attend_2/pallas_call | solution.py:365
  101.0 3.8 %collective-permute-start.12 = (bf16[144,640]{1,0:T(8,128)(2,1)S(1)}, bf16[144,640]{1,0:T(8,128)(2,1)S(1)}, u32[]{:S(2)}, u32[]{:S(2)}) collective-permute-start(bf16[144,640]{1,0:T(8,128)(2,1)S(1)} %get-tuple-element.44.refs_9_), channel_id=1, source_target_pairs={{0,6},{2,0},{4,2},{6,4},{1,7},{3,1},{5,3},{7,5},{8,14},{10,8},{12,... | collective-permute-start | bytes 552968 | tf_op jit(solution)/shard_map/ppermute | solution.py:421
  104.9 0.0 collective-permute-start.13
  104.9 1.0 collective-permute-start.14
  105.8 5.4 %attend_3.1.refs_0_ = bf16[144,640]{1,0:T(8,128)(2,1)S(1)} custom-call(bf16[6,272,128]{2,1,0:T(8,128)(2,1)S(1)} %get-tuple-element.40.refs_0_, bf16[6,272,128]{2,1,0:T(8,128)(2,1)S(1)} %get-tuple-element.41.refs_1_, bf16[6,272,128]{2,1,0:T(8,128)(2,1)S(1)} %collective-permute-done.10.refs_2_, bf16[6,272,128]{2,1,0:T(8,128)(2,1)S(1)} %collective-permute-done.11.refs_3_, ...), custom_call_target="tpu_custom_call" | custom-call | flops 2013265920 | bytes 1572864 | tf_op jit(solution)/shard_map/attend_3/pallas_call | solution.py:365
  111.3 1.1 collective-permute-done.12.refs_1_
  112.3 1.6 %collective-permute-done.13.refs_2_ = bf16[144,640]{1,0:T(8,128)(2,1)S(1)} collective-permute-done((bf16[144,640]{1,0:T(8,128)(2,1)S(1)}, bf16[144,640]{1,0:T(8,128)(2,1)S(1)}, u32[]{:S(2)}, u32[]{:S(2)}) %collective-permute-start.13) | collective-permute-done | bytes 184352 | tf_op jit(solution)/shard_map/ppermute | solution.py:421
  114.0 1.8 %collective-permute-done.14.refs_3_ = bf16[144,640]{1,0:T(8,128)(2,1)S(1)} collective-permute-done((bf16[144,640]{1,0:T(8,128)(2,1)S(1)}, bf16[144,640]{1,0:T(8,128)(2,1)S(1)}, u32[]{:S(2)}, u32[]{:S(2)}) %collective-permute-start.14) | collective-permute-done | bytes 184352 | tf_op jit(solution)/shard_map/ppermute | solution.py:421
  115.7 1.3 %combine.1 = bf16[128,640]{1,0:T(8,128)(2,1)} custom-call(bf16[144,640]{1,0:T(8,128)(2,1)S(1)} %attend_3.1.refs_0_, bf16[144,640]{1,0:T(8,128)(2,1)S(1)} %collective-permute-done.12.refs_1_, bf16[144,640]{1,0:T(8,128)(2,1)S(1)} %collective-permute-done.13.refs_2_, bf16[144,640]{1,0:T(8,128)(2,1)S(1)} %collective-permute-done.14.refs_3_), custom_call_target="tpu_custom_call" | custom-call | tf_op jit(solution)/shard_map/combine/pallas_call | solution.py:410
  (3 shorter events, 0.0 us)
Async XLA Ops:
  2.0 29.0 %copy-start = (bf16[144,640]{1,0:T(8,128)(2,1)S(1)}, bf16[144,640]{1,0:T(8,128)(2,1)}, u32[]{:S(2)}) copy-start(bf16[144,640]{1,0:T(8,128)(2,1)} %get-tuple-element.26.refs_3_) | copy-start | bytes 552964
  2.0 26.8 %all-to-all-start = ((bf16[8,272,128]{2,1,0:T(8,128)(2,1)}), bf16[8,272,128]{2,1,0:T(8,128)(2,1)S(1)}, u32[]{:S(2)}, u32[]{:S(2)}) async-start(bf16[8,272,128]{2,1,0:T(8,128)(2,1)} %get-tuple-element.27), calls=%async_computation | async-start | bytes 1114112 | tf_op jit(solution)/shard_map/all_to_all | solution.py:528
  10.6 7.9 %collective-permute-start = (bf16[144,640]{1,0:T(8,128)(2,1)}, bf16[144,640]{1,0:T(8,128)(2,1)S(1)}, u32[]{:S(2)}, u32[]{:S(2)}) collective-permute-start(bf16[144,640]{1,0:T(8,128)(2,1)} %get-tuple-element.26.refs_3_), channel_id=1, source_target_pairs={{0,2},{2,4},{4,6},{6,0},{1,3},{3,5},{5,7},{7,1},{8,10},{10,12},{12... | collective-permute-start | bytes 552968 | tf_op jit(solution)/shard_map/ppermute | solution.py:421
  12.2 11.1 %collective-permute-start.1 = (bf16[144,640]{1,0:T(8,128)(2,1)}, bf16[144,640]{1,0:T(8,128)(2,1)S(1)}, u32[]{:S(2)}, u32[]{:S(2)}) collective-permute-start(bf16[144,640]{1,0:T(8,128)(2,1)} %get-tuple-element.26.refs_3_), channel_id=1, source_target_pairs={{0,4},{2,6},{4,0},{6,2},{1,5},{3,7},{5,1},{7,3},{8,12},{10,14},{12... | collective-permute-start | bytes 552968 | tf_op jit(solution)/shard_map/ppermute | solution.py:421
  15.1 8.2 %collective-permute-start.2 = (bf16[144,640]{1,0:T(8,128)(2,1)}, bf16[144,640]{1,0:T(8,128)(2,1)S(1)}, u32[]{:S(2)}, u32[]{:S(2)}) collective-permute-start(bf16[144,640]{1,0:T(8,128)(2,1)} %get-tuple-element.26.refs_3_), channel_id=1, source_target_pairs={{0,6},{2,0},{4,2},{6,4},{1,7},{3,1},{5,3},{7,5},{8,14},{10,8},{12,... | collective-permute-start | bytes 552968 | tf_op jit(solution)/shard_map/ppermute | solution.py:421
  28.8 2.2 %collective-permute-start.3 = (bf16[8,272,128]{2,1,0:T(8,128)(2,1)S(1)}, bf16[8,272,128]{2,1,0:T(8,128)(2,1)S(1)}, u32[]{:S(2)}, u32[]{:S(2)}) collective-permute-start(bf16[8,272,128]{2,1,0:T(8,128)(2,1)S(1)} %after.3.refs_4_.refs_0_), channel_id=1, source_target_pairs={{0,64},{64,0},{1,65},{65,1},{2,66},{66,2},{3,67},{67,3},{4,68},{68... | collective-permute-start | bytes 1671176 | tf_op jit(solution)/shard_map/ppermute | solution.py:421
  28.9 45.6 %collective-permute-start.4 = (bf16[6,272,128]{2,1,0:T(8,128)(2,1)S(1)}, bf16[6,272,128]{2,1,0:T(8,128)(2,1)S(1)}, u32[]{:S(2)}, u32[]{:S(2)}) collective-permute-start(bf16[6,272,128]{2,1,0:T(8,128)(2,1)S(1)} %get-tuple-element.29), channel_id=1, source_target_pairs={{0,128},{128,1},{1,129},{129,0},{2,130},{130,3},{3,131},{131,2},{4... | collective-permute-start | bytes 1253384 | tf_op jit(solution)/shard_map/ppermute | solution.py:526
  29.4 45.0 %collective-permute-start.5 = (bf16[6,272,128]{2,1,0:T(8,128)(2,1)S(1)}, bf16[6,272,128]{2,1,0:T(8,128)(2,1)S(1)}, u32[]{:S(2)}, u32[]{:S(2)}) collective-permute-start(bf16[6,272,128]{2,1,0:T(8,128)(2,1)S(1)} %get-tuple-element.30), channel_id=1, source_target_pairs={{128,0},{1,128},{129,1},{0,129},{130,2},{3,130},{131,3},{2,131},{1... | collective-permute-start | bytes 1253384 | tf_op jit(solution)/shard_map/ppermute | solution.py:526
  74.5 2.9 %collective-permute-start.6 = (bf16[6,272,128]{2,1,0:T(8,128)(2,1)S(1)}, bf16[6,272,128]{2,1,0:T(8,128)(2,1)S(1)}, u32[]{:S(2)}, u32[]{:S(2)}) collective-permute-start(bf16[6,272,128]{2,1,0:T(8,128)(2,1)S(1)} %get-tuple-element.31.refs_0_.refs_1_), channel_id=1, source_target_pairs={{0,64},{64,0},{1,65},{65,1},{2,66},{66,2},{3,67},{67,3},{4,68},{68... | collective-permute-start | bytes 1253384 | tf_op jit(solution)/shard_map/ppermute | solution.py:421
  74.6 2.8 %collective-permute-start.7 = (bf16[6,272,128]{2,1,0:T(8,128)(2,1)S(1)}, bf16[6,272,128]{2,1,0:T(8,128)(2,1)S(1)}, u32[]{:S(2)}, u32[]{:S(2)}) collective-permute-start(bf16[6,272,128]{2,1,0:T(8,128)(2,1)S(1)} %get-tuple-element.32.refs_1_.refs_2_), channel_id=1, source_target_pairs={{0,64},{64,0},{1,65},{65,1},{2,66},{66,2},{3,67},{67,3},{4,68},{68... | collective-permute-start | bytes 1253384 | tf_op jit(solution)/shard_map/ppermute | solution.py:421
  75.1 12.4 %collective-permute-start.8 = (bf16[6,272,128]{2,1,0:T(8,128)(2,1)S(1)}, bf16[6,272,128]{2,1,0:T(8,128)(2,1)S(1)}, u32[]{:S(2)}, u32[]{:S(2)}) collective-permute-start(bf16[6,272,128]{2,1,0:T(8,128)(2,1)S(1)} %get-tuple-element.38), channel_id=1, source_target_pairs={{0,128},{128,1},{1,129},{129,0},{2,130},{130,3},{3,131},{131,2},{4... | collective-permute-start | bytes 1253384 | tf_op jit(solution)/shard_map/ppermute | solution.py:526
  76.6 12.9 %collective-permute-start.9 = (bf16[6,272,128]{2,1,0:T(8,128)(2,1)S(1)}, bf16[6,272,128]{2,1,0:T(8,128)(2,1)S(1)}, u32[]{:S(2)}, u32[]{:S(2)}) collective-permute-start(bf16[6,272,128]{2,1,0:T(8,128)(2,1)S(1)} %get-tuple-element.39), channel_id=1, source_target_pairs={{128,0},{1,128},{129,1},{0,129},{130,2},{3,130},{131,3},{2,131},{1... | collective-permute-start | bytes 1253384 | tf_op jit(solution)/shard_map/ppermute | solution.py:526
  89.5 1.8 %collective-permute-start.10 = (bf16[6,272,128]{2,1,0:T(8,128)(2,1)S(1)}, bf16[6,272,128]{2,1,0:T(8,128)(2,1)S(1)}, u32[]{:S(2)}, u32[]{:S(2)}) collective-permute-start(bf16[6,272,128]{2,1,0:T(8,128)(2,1)S(1)} %get-tuple-element.40.refs_0_), channel_id=1, source_target_pairs={{0,64},{64,0},{1,65},{65,1},{2,66},{66,2},{3,67},{67,3},{4,68},{68... | collective-permute-start | bytes 1253384 | tf_op jit(solution)/shard_map/ppermute | solution.py:421
  89.5 2.4 %collective-permute-start.11 = (bf16[6,272,128]{2,1,0:T(8,128)(2,1)S(1)}, bf16[6,272,128]{2,1,0:T(8,128)(2,1)S(1)}, u32[]{:S(2)}, u32[]{:S(2)}) collective-permute-start(bf16[6,272,128]{2,1,0:T(8,128)(2,1)S(1)} %get-tuple-element.41.refs_1_), channel_id=1, source_target_pairs={{0,64},{64,0},{1,65},{65,1},{2,66},{66,2},{3,67},{67,3},{4,68},{68... | collective-permute-start | bytes 1253384 | tf_op jit(solution)/shard_map/ppermute | solution.py:421
  101.0 11.3 %collective-permute-start.12 = (bf16[144,640]{1,0:T(8,128)(2,1)S(1)}, bf16[144,640]{1,0:T(8,128)(2,1)S(1)}, u32[]{:S(2)}, u32[]{:S(2)}) collective-permute-start(bf16[144,640]{1,0:T(8,128)(2,1)S(1)} %get-tuple-element.44.refs_9_), channel_id=1, source_target_pairs={{0,6},{2,0},{4,2},{6,4},{1,7},{3,1},{5,3},{7,5},{8,14},{10,8},{12,... | collective-permute-start | bytes 552968 | tf_op jit(solution)/shard_map/ppermute | solution.py:421
  104.9 9.1 %collective-permute-start.13 = (bf16[144,640]{1,0:T(8,128)(2,1)S(1)}, bf16[144,640]{1,0:T(8,128)(2,1)S(1)}, u32[]{:S(2)}, u32[]{:S(2)}) collective-permute-start(bf16[144,640]{1,0:T(8,128)(2,1)S(1)} %get-tuple-element.45), channel_id=1, source_target_pairs={{0,4},{2,6},{4,0},{6,2},{1,5},{3,7},{5,1},{7,3},{8,12},{10,14},{12... | collective-permute-start | bytes 552968 | tf_op jit(solution)/shard_map/ppermute | solution.py:421
  104.9 10.9 %collective-permute-start.14 = (bf16[144,640]{1,0:T(8,128)(2,1)S(1)}, bf16[144,640]{1,0:T(8,128)(2,1)S(1)}, u32[]{:S(2)}, u32[]{:S(2)}) collective-permute-start(bf16[144,640]{1,0:T(8,128)(2,1)S(1)} %get-tuple-element.46), channel_id=1, source_target_pairs={{0,2},{2,4},{4,6},{6,0},{1,3},{3,5},{5,7},{7,1},{8,10},{10,12},{12... | collective-permute-start | bytes 552968 | tf_op jit(solution)/shard_map/ppermute | solution.py:421

commit v2 on v1

--- a/solution.py
+++ b/solution.py
@@ -526,9 +526,9 @@
         return [lax.ppermute(up, ("xl", "xh"), step), lax.ppermute(down, ("xl", "xh"), back)]
 
     own = lax.all_to_all(kv, "z", 0, 0)
-    q1, q2, q3 = (shift(qn, "y", 4, k) for k in (1, 2, 3))
+    q2, q1, q3 = (shift(qn, "y", 4, k) for k in (2, 1, 3))
     queries = [q1, q2, q3, qn]
-    (own,) = after([own], [q1, q2, q3])
+    (own,) = after([own], [q2, q1, q3])
     one = pass_on(*pick([own], [[(0, 0, 6)], [(0, 2, 8)]]))
     own_c = swap([own])
     state = attend(queries, [own] + own_c, (), "attend_0")
@@ -540,7 +540,9 @@
     rest = two + swap(two)
     outs = attend(queries, rest, state, "attend_2", ys=(0, 1, 2))
     (mine,) = attend(queries, rest, state, "attend_3", ys=(3,), wait=outs[:1])
-    return combine([mine] + [shift(o, "y", 4, -k) for k, o in zip((1, 2, 3), outs)])
+    o1, o2, o3 = outs
+    r2, r1, r3 = shift(o2, "y", 4, -2), shift(o1, "y", 4, -1), shift(o3, "y", 4, -3)
+    return combine([mine, r2, r1, r3])
 
 
 def solution(mesh):

time: 117 us -> 116 us (level)
  the two profiles are of different devices: /device:TPU:6 before, /device:TPU:1 now
where the time goes in v2:
time: 116 us; the launch traced here: 115 us
  Pallas kernels  70.2 us (61%)
  starting transfers between devices  26.4 us (23%)
  waiting for transfers between devices  17.8 us (15%)
    pallas_call x4, Pallas kernels, attend(): pl.pallas_call(functools.partial(attend_kernel, first, ys, len(blocks), l...  66.9 us
    ppermute x11, starting transfers between devices, shift(): return lax.ppermute(x, axis, [(i, (i + by) % n) for i in range(n)])  11.5 us
    ppermute x11, waiting for transfers between devices, shift(): return lax.ppermute(x, axis, [(i, (i + by) % n) for i in range(n)])  11 us
    all_to_all x1, starting transfers between devices, local(): own = lax.all_to_all(kv, 'z', 0, 0)  9.16 us
    all_to_all x1, waiting for transfers between devices, local(): own = lax.all_to_all(kv, 'z', 0, 0)  6.85 us
    ppermute x2, starting transfers between devices, pass_on(): lax.ppermute(down, ('xl', 'xh'), back)  4.13 us
  transfers between devices with their start and end apart: 16, of which 7 were waited for; matrix products, arithmetic and copies ran while one was open for 0% of the time, Pallas kernels for 51%

profile of v2, /device:TPU:1, one launch (start us, length us, event | category | flops | bytes accessed | tf_op | source)
XLA Modules:
  0.0 114.6 jit_solution(6896432874214565413)
XLA Ops:
  0.0 1.9 %pack.1 = (bf16[8,272,128]{2,1,0:T(8,128)(2,1)}, bf16[144,640]{1,0:T(8,128)(2,1)}) custom-call(s32[128]{0:T(128)} %place_hbm.1, bf16[128,640]{1,0:T(8,128)(2,1)} %q_hbm.1, bf16[128,128]{1,0:T(8,128)(2,1)} %k_hbm.1, bf16[128,128]{1,0:T(8,128)(2,1)} %v_hbm.1), custom_call_target="tpu_custom_call" | custom-call | tf_op jit(solution)/shard_map/pack/pallas_call | solution.py:474
  2.0 0.0 copy-start
  2.0 9.2 %all-to-all-start = ((bf16[8,272,128]{2,1,0:T(8,128)(2,1)}), bf16[8,272,128]{2,1,0:T(8,128)(2,1)S(1)}, u32[]{:S(2)}, u32[]{:S(2)}) async-start(bf16[8,272,128]{2,1,0:T(8,128)(2,1)} %get-tuple-element.27), calls=%async_computation | async-start | bytes 1114112 | tf_op jit(solution)/shard_map/all_to_all | solution.py:528
  11.1 1.3 %collective-permute-start = (bf16[144,640]{1,0:T(8,128)(2,1)}, bf16[144,640]{1,0:T(8,128)(2,1)S(1)}, u32[]{:S(2)}, u32[]{:S(2)}) collective-permute-start(bf16[144,640]{1,0:T(8,128)(2,1)} %get-tuple-element.26.refs_3_), channel_id=1, source_target_pairs={{0,2},{2,4},{4,6},{6,0},{1,3},{3,5},{5,7},{7,1},{8,10},{10,12},{12... | collective-permute-start | bytes 552968 | tf_op jit(solution)/shard_map/ppermute | solution.py:421
  12.4 2.6 %collective-permute-start.1 = (bf16[144,640]{1,0:T(8,128)(2,1)}, bf16[144,640]{1,0:T(8,128)(2,1)S(1)}, u32[]{:S(2)}, u32[]{:S(2)}) collective-permute-start(bf16[144,640]{1,0:T(8,128)(2,1)} %get-tuple-element.26.refs_3_), channel_id=1, source_target_pairs={{0,4},{2,6},{4,0},{6,2},{1,5},{3,7},{5,1},{7,3},{8,12},{10,14},{12... | collective-permute-start | bytes 552968 | tf_op jit(solution)/shard_map/ppermute | solution.py:421
  15.0 1.1 collective-permute-start.2
  16.1 1.7 %collective-permute-done.refs_1_.refs_0_ = bf16[144,640]{1,0:T(8,128)(2,1)S(1)} collective-permute-done((bf16[144,640]{1,0:T(8,128)(2,1)}, bf16[144,640]{1,0:T(8,128)(2,1)S(1)}, u32[]{:S(2)}, u32[]{:S(2)}) %collective-permute-start) | collective-permute-done | bytes 184352 | tf_op jit(solution)/shard_map/ppermute | solution.py:421
  17.9 5.1 %collective-permute-done.1.refs_0_.refs_1_ = bf16[144,640]{1,0:T(8,128)(2,1)S(1)} collective-permute-done((bf16[144,640]{1,0:T(8,128)(2,1)}, bf16[144,640]{1,0:T(8,128)(2,1)S(1)}, u32[]{:S(2)}, u32[]{:S(2)}) %collective-permute-start.1) | collective-permute-done | bytes 184352 | tf_op jit(solution)/shard_map/ppermute | solution.py:421
  22.9 0.0 collective-permute-done.2.refs_2_
  22.9 6.9 %all-to-all-done.refs_3_ = bf16[8,272,128]{2,1,0:T(8,128)(2,1)S(1)} async-done(((bf16[8,272,128]{2,1,0:T(8,128)(2,1)}), bf16[8,272,128]{2,1,0:T(8,128)(2,1)S(1)}, u32[]{:S(2)}, u32[]{:S(2)}) %all-to-all-start) | async-done | bytes 557088 | tf_op jit(solution)/shard_map/all_to_all | solution.py:528
  29.8 0.5 collective-permute-start.3
  30.3 0.1 pick.2
  30.4 1.3 %collective-permute-start.4 = (bf16[6,272,128]{2,1,0:T(8,128)(2,1)S(1)}, bf16[6,272,128]{2,1,0:T(8,128)(2,1)S(1)}, u32[]{:S(2)}, u32[]{:S(2)}) collective-permute-start(bf16[6,272,128]{2,1,0:T(8,128)(2,1)S(1)} %get-tuple-element.29), channel_id=1, source_target_pairs={{0,128},{128,1},{1,129},{129,0},{2,130},{130,3},{3,131},{131,2},{4... | collective-permute-start | bytes 1253384 | tf_op jit(solution)/shard_map/ppermute | solution.py:526
  31.7 1.5 %collective-permute-start.5 = (bf16[6,272,128]{2,1,0:T(8,128)(2,1)S(1)}, bf16[6,272,128]{2,1,0:T(8,128)(2,1)S(1)}, u32[]{:S(2)}, u32[]{:S(2)}) collective-permute-start(bf16[6,272,128]{2,1,0:T(8,128)(2,1)S(1)} %get-tuple-element.30), channel_id=1, source_target_pairs={{128,0},{1,128},{129,1},{0,129},{130,2},{3,130},{131,3},{2,131},{1... | collective-permute-start | bytes 1253384 | tf_op jit(solution)/shard_map/ppermute | solution.py:526
  33.1 0.0 collective-permute-done.3.refs_5_
  33.1 0.0 copy-done
  33.1 42.8 %attend_0.1 = (s32[8]{0:T(128)S(1)}, f32[8,128]{1,0:T(8,128)S(1)}, bf16[11,128,256]{2,1,0:T(8,128)(2,1)S(1)}, f32[11,144,256]{2,1,0:T(8,128)S(1)}, f32[11,1,256]{2,1,0:T(1,128)S(1)}) custom-call(bf16[144,640]{1,0:T(8,128)(2,1)S(1)} %collective-permute-done.refs_1_.refs_0_, bf16[144,640]{1,0:T(8,128)(2,1)S(1)} %collective-permute-done.1.refs_0_.refs_1_, ...), custom_call_target="tpu_custom_call" | custom-call | flops 1342177280 | bytes 1048576 | tf_op jit(solution)/shard_map/attend_0/pallas_call | solution.py:365
  75.9 0.0 collective-permute-done.4.refs_1_
  76.0 0.0 collective-permute-done.5.refs_2_
  76.0 0.7 collective-permute-start.6
  76.6 0.1 collective-permute-start.7
  76.7 0.1 pick.3
  76.8 0.3 collective-permute-start.8
  77.1 2.7 %collective-permute-start.9 = (bf16[6,272,128]{2,1,0:T(8,128)(2,1)S(1)}, bf16[6,272,128]{2,1,0:T(8,128)(2,1)S(1)}, u32[]{:S(2)}, u32[]{:S(2)}) collective-permute-start(bf16[6,272,128]{2,1,0:T(8,128)(2,1)S(1)} %get-tuple-element.39), channel_id=1, source_target_pairs={{128,0},{1,128},{129,1},{0,129},{130,2},{3,130},{131,3},{2,131},{1... | collective-permute-start | bytes 1253384 | tf_op jit(solution)/shard_map/ppermute | solution.py:526
  79.7 0.0 collective-permute-done.6.refs_2_
  79.7 0.0 collective-permute-done.7.refs_3_
  79.7 9.6 %attend_1.1 = (s32[8]{0:T(128)S(1)}, f32[11,144,256]{2,1,0:T(8,128)S(1)}, f32[11,1,256]{2,1,0:T(1,128)S(1)}) custom-call(bf16[6,272,128]{2,1,0:T(8,128)(2,1)S(1)} %get-tuple-element.31.refs_0_.refs_1_, bf16[6,272,128]{2,1,0:T(8,128)(2,1)S(1)} %get-tuple-element.32.refs_1_.refs_2_, bf16[6,272,128]{2,1,0:T(8,128)(2,1)S(1)} %collective-permute-done.6.refs_2_, ...), custom_call_target="tpu_custom_call" | custom-call | flops 2013265920 | bytes 1572864 | tf_op jit(solution)/shard_map/attend_1/pallas_call | solution.py:365
  89.4 0.0 collective-permute-done.8.refs_1_
  89.4 0.0 collective-permute-done.9.refs_2_
  89.4 0.9 collective-permute-start.10
  90.3 0.1 collective-permute-start.11
  90.4 1.3 %collective-permute-done.10.refs_2_ = bf16[6,272,128]{2,1,0:T(8,128)(2,1)S(1)} collective-permute-done((bf16[6,272,128]{2,1,0:T(8,128)(2,1)S(1)}, bf16[6,272,128]{2,1,0:T(8,128)(2,1)S(1)}, u32[]{:S(2)}, u32[]{:S(2)}) %collective-permute-start.10) | collective-permute-done | bytes 417824 | tf_op jit(solution)/shard_map/ppermute | solution.py:421
  91.7 0.6 collective-permute-done.11.refs_3_
  92.3 8.8 %attend_2.1 = (bf16[144,640]{1,0:T(8,128)(2,1)S(1)}, bf16[144,640]{1,0:T(8,128)(2,1)S(1)}, bf16[144,640]{1,0:T(8,128)(2,1)S(1)}) custom-call(bf16[6,272,128]{2,1,0:T(8,128)(2,1)S(1)} %get-tuple-element.40.refs_0_, bf16[6,272,128]{2,1,0:T(8,128)(2,1)S(1)} %get-tuple-element.41.refs_1_, bf16[6,272,128]{2,1,0:T(8,128)(2,1)S(1)} %collective-permute-done.10.refs_2_, ...), custom_call_target="tpu_custom_call" | custom-call | flops 2013265920 | bytes 1572864 | tf_op jit(solution)/shard_map/attend_2/pallas_call | solution.py:365
  101.1 2.8 %collective-permute-start.12 = (bf16[144,640]{1,0:T(8,128)(2,1)S(1)}, bf16[144,640]{1,0:T(8,128)(2,1)S(1)}, u32[]{:S(2)}, u32[]{:S(2)}) collective-permute-start(bf16[144,640]{1,0:T(8,128)(2,1)S(1)} %get-tuple-element.45), channel_id=1, source_target_pairs={{0,4},{2,6},{4,0},{6,2},{1,5},{3,7},{5,1},{7,3},{8,12},{10,14},{12... | collective-permute-start | bytes 552968 | tf_op jit(solution)/shard_map/ppermute | solution.py:421
  104.0 0.8 collective-permute-start.13
  104.8 0.7 collective-permute-start.14
  105.5 5.6 %attend_3.1.refs_0_ = bf16[144,640]{1,0:T(8,128)(2,1)S(1)} custom-call(bf16[6,272,128]{2,1,0:T(8,128)(2,1)S(1)} %get-tuple-element.40.refs_0_, bf16[6,272,128]{2,1,0:T(8,128)(2,1)S(1)} %get-tuple-element.41.refs_1_, bf16[6,272,128]{2,1,0:T(8,128)(2,1)S(1)} %collective-permute-done.10.refs_2_, bf16[6,272,128]{2,1,0:T(8,128)(2,1)S(1)} %collective-permute-done.11.refs_3_, ...), custom_call_target="tpu_custom_call" | custom-call | flops 2013265920 | bytes 1572864 | tf_op jit(solution)/shard_map/attend_3/pallas_call | solution.py:365
  111.1 0.0 collective-permute-done.12.refs_1_
  111.1 1.8 %collective-permute-done.13.refs_2_ = bf16[144,640]{1,0:T(8,128)(2,1)S(1)} collective-permute-done((bf16[144,640]{1,0:T(8,128)(2,1)S(1)}, bf16[144,640]{1,0:T(8,128)(2,1)S(1)}, u32[]{:S(2)}, u32[]{:S(2)}) %collective-permute-start.13) | collective-permute-done | bytes 184352 | tf_op jit(solution)/shard_map/ppermute | solution.py:421
  112.9 0.4 collective-permute-done.14.refs_3_
  113.3 1.3 %combine.1 = bf16[128,640]{1,0:T(8,128)(2,1)} custom-call(bf16[144,640]{1,0:T(8,128)(2,1)S(1)} %attend_3.1.refs_0_, bf16[144,640]{1,0:T(8,128)(2,1)S(1)} %collective-permute-done.12.refs_1_, bf16[144,640]{1,0:T(8,128)(2,1)S(1)} %collective-permute-done.13.refs_2_, bf16[144,640]{1,0:T(8,128)(2,1)S(1)} %collective-permute-done.14.refs_3_), custom_call_target="tpu_custom_call" | custom-call | tf_op jit(solution)/shard_map/combine/pallas_call | solution.py:410
  (3 shorter events, 0.0 us)
Async XLA Ops:
  2.0 31.2 %copy-start = (bf16[144,640]{1,0:T(8,128)(2,1)S(1)}, bf16[144,640]{1,0:T(8,128)(2,1)}, u32[]{:S(2)}) copy-start(bf16[144,640]{1,0:T(8,128)(2,1)} %get-tuple-element.26.refs_3_) | copy-start | bytes 552964
  2.0 27.8 %all-to-all-start = ((bf16[8,272,128]{2,1,0:T(8,128)(2,1)}), bf16[8,272,128]{2,1,0:T(8,128)(2,1)S(1)}, u32[]{:S(2)}, u32[]{:S(2)}) async-start(bf16[8,272,128]{2,1,0:T(8,128)(2,1)} %get-tuple-element.27), calls=%async_computation | async-start | bytes 1114112 | tf_op jit(solution)/shard_map/all_to_all | solution.py:528
  11.1 6.7 %collective-permute-start = (bf16[144,640]{1,0:T(8,128)(2,1)}, bf16[144,640]{1,0:T(8,128)(2,1)S(1)}, u32[]{:S(2)}, u32[]{:S(2)}) collective-permute-start(bf16[144,640]{1,0:T(8,128)(2,1)} %get-tuple-element.26.refs_3_), channel_id=1, source_target_pairs={{0,2},{2,4},{4,6},{6,0},{1,3},{3,5},{5,7},{7,1},{8,10},{10,12},{12... | collective-permute-start | bytes 552968 | tf_op jit(solution)/shard_map/ppermute | solution.py:421
  12.4 10.5 %collective-permute-start.1 = (bf16[144,640]{1,0:T(8,128)(2,1)}, bf16[144,640]{1,0:T(8,128)(2,1)S(1)}, u32[]{:S(2)}, u32[]{:S(2)}) collective-permute-start(bf16[144,640]{1,0:T(8,128)(2,1)} %get-tuple-element.26.refs_3_), channel_id=1, source_target_pairs={{0,4},{2,6},{4,0},{6,2},{1,5},{3,7},{5,1},{7,3},{8,12},{10,14},{12... | collective-permute-start | bytes 552968 | tf_op jit(solution)/shard_map/ppermute | solution.py:421
  15.0 7.9 %collective-permute-start.2 = (bf16[144,640]{1,0:T(8,128)(2,1)}, bf16[144,640]{1,0:T(8,128)(2,1)S(1)}, u32[]{:S(2)}, u32[]{:S(2)}) collective-permute-start(bf16[144,640]{1,0:T(8,128)(2,1)} %get-tuple-element.26.refs_3_), channel_id=1, source_target_pairs={{0,6},{2,0},{4,2},{6,4},{1,7},{3,1},{5,3},{7,5},{8,14},{10,8},{12,... | collective-permute-start | bytes 552968 | tf_op jit(solution)/shard_map/ppermute | solution.py:421
  29.8 3.3 %collective-permute-start.3 = (bf16[8,272,128]{2,1,0:T(8,128)(2,1)S(1)}, bf16[8,272,128]{2,1,0:T(8,128)(2,1)S(1)}, u32[]{:S(2)}, u32[]{:S(2)}) collective-permute-start(bf16[8,272,128]{2,1,0:T(8,128)(2,1)S(1)} %after.3.refs_4_.refs_0_), channel_id=1, source_target_pairs={{0,64},{64,0},{1,65},{65,1},{2,66},{66,2},{3,67},{67,3},{4,68},{68... | collective-permute-start | bytes 1671176 | tf_op jit(solution)/shard_map/ppermute | solution.py:421
  30.4 45.6 %collective-permute-start.4 = (bf16[6,272,128]{2,1,0:T(8,128)(2,1)S(1)}, bf16[6,272,128]{2,1,0:T(8,128)(2,1)S(1)}, u32[]{:S(2)}, u32[]{:S(2)}) collective-permute-start(bf16[6,272,128]{2,1,0:T(8,128)(2,1)S(1)} %get-tuple-element.29), channel_id=1, source_target_pairs={{0,128},{128,1},{1,129},{129,0},{2,130},{130,3},{3,131},{131,2},{4... | collective-permute-start | bytes 1253384 | tf_op jit(solution)/shard_map/ppermute | solution.py:526
  31.7 44.3 %collective-permute-start.5 = (bf16[6,272,128]{2,1,0:T(8,128)(2,1)S(1)}, bf16[6,272,128]{2,1,0:T(8,128)(2,1)S(1)}, u32[]{:S(2)}, u32[]{:S(2)}) collective-permute-start(bf16[6,272,128]{2,1,0:T(8,128)(2,1)S(1)} %get-tuple-element.30), channel_id=1, source_target_pairs={{128,0},{1,128},{129,1},{0,129},{130,2},{3,130},{131,3},{2,131},{1... | collective-permute-start | bytes 1253384 | tf_op jit(solution)/shard_map/ppermute | solution.py:526
  76.0 3.8 %collective-permute-start.6 = (bf16[6,272,128]{2,1,0:T(8,128)(2,1)S(1)}, bf16[6,272,128]{2,1,0:T(8,128)(2,1)S(1)}, u32[]{:S(2)}, u32[]{:S(2)}) collective-permute-start(bf16[6,272,128]{2,1,0:T(8,128)(2,1)S(1)} %get-tuple-element.31.refs_0_.refs_1_), channel_id=1, source_target_pairs={{0,64},{64,0},{1,65},{65,1},{2,66},{66,2},{3,67},{67,3},{4,68},{68... | collective-permute-start | bytes 1253384 | tf_op jit(solution)/shard_map/ppermute | solution.py:421
  76.6 3.1 %collective-permute-start.7 = (bf16[6,272,128]{2,1,0:T(8,128)(2,1)S(1)}, bf16[6,272,128]{2,1,0:T(8,128)(2,1)S(1)}, u32[]{:S(2)}, u32[]{:S(2)}) collective-permute-start(bf16[6,272,128]{2,1,0:T(8,128)(2,1)S(1)} %get-tuple-element.32.refs_1_.refs_2_), channel_id=1, source_target_pairs={{0,64},{64,0},{1,65},{65,1},{2,66},{66,2},{3,67},{67,3},{4,68},{68... | collective-permute-start | bytes 1253384 | tf_op jit(solution)/shard_map/ppermute | solution.py:421
  76.8 12.6 %collective-permute-start.8 = (bf16[6,272,128]{2,1,0:T(8,128)(2,1)S(1)}, bf16[6,272,128]{2,1,0:T(8,128)(2,1)S(1)}, u32[]{:S(2)}, u32[]{:S(2)}) collective-permute-start(bf16[6,272,128]{2,1,0:T(8,128)(2,1)S(1)} %get-tuple-element.38), channel_id=1, source_target_pairs={{0,128},{128,1},{1,129},{129,0},{2,130},{130,3},{3,131},{131,2},{4... | collective-permute-start | bytes 1253384 | tf_op jit(solution)/shard_map/ppermute | solution.py:526
  77.1 12.3 %collective-permute-start.9 = (bf16[6,272,128]{2,1,0:T(8,128)(2,1)S(1)}, bf16[6,272,128]{2,1,0:T(8,128)(2,1)S(1)}, u32[]{:S(2)}, u32[]{:S(2)}) collective-permute-start(bf16[6,272,128]{2,1,0:T(8,128)(2,1)S(1)} %get-tuple-element.39), channel_id=1, source_target_pairs={{128,0},{1,128},{129,1},{0,129},{130,2},{3,130},{131,3},{2,131},{1... | collective-permute-start | bytes 1253384 | tf_op jit(solution)/shard_map/ppermute | solution.py:526
  89.4 2.3 %collective-permute-start.10 = (bf16[6,272,128]{2,1,0:T(8,128)(2,1)S(1)}, bf16[6,272,128]{2,1,0:T(8,128)(2,1)S(1)}, u32[]{:S(2)}, u32[]{:S(2)}) collective-permute-start(bf16[6,272,128]{2,1,0:T(8,128)(2,1)S(1)} %get-tuple-element.40.refs_0_), channel_id=1, source_target_pairs={{0,64},{64,0},{1,65},{65,1},{2,66},{66,2},{3,67},{67,3},{4,68},{68... | collective-permute-start | bytes 1253384 | tf_op jit(solution)/shard_map/ppermute | solution.py:421
  90.3 2.0 %collective-permute-start.11 = (bf16[6,272,128]{2,1,0:T(8,128)(2,1)S(1)}, bf16[6,272,128]{2,1,0:T(8,128)(2,1)S(1)}, u32[]{:S(2)}, u32[]{:S(2)}) collective-permute-start(bf16[6,272,128]{2,1,0:T(8,128)(2,1)S(1)} %get-tuple-element.41.refs_1_), channel_id=1, source_target_pairs={{0,64},{64,0},{1,65},{65,1},{2,66},{66,2},{3,67},{67,3},{4,68},{68... | collective-permute-start | bytes 1253384 | tf_op jit(solution)/shard_map/ppermute | solution.py:421
  101.1 9.9 %collective-permute-start.12 = (bf16[144,640]{1,0:T(8,128)(2,1)S(1)}, bf16[144,640]{1,0:T(8,128)(2,1)S(1)}, u32[]{:S(2)}, u32[]{:S(2)}) collective-permute-start(bf16[144,640]{1,0:T(8,128)(2,1)S(1)} %get-tuple-element.45), channel_id=1, source_target_pairs={{0,4},{2,6},{4,0},{6,2},{1,5},{3,7},{5,1},{7,3},{8,12},{10,14},{12... | collective-permute-start | bytes 552968 | tf_op jit(solution)/shard_map/ppermute | solution.py:421
  104.0 8.9 %collective-permute-start.13 = (bf16[144,640]{1,0:T(8,128)(2,1)S(1)}, bf16[144,640]{1,0:T(8,128)(2,1)S(1)}, u32[]{:S(2)}, u32[]{:S(2)}) collective-permute-start(bf16[144,640]{1,0:T(8,128)(2,1)S(1)} %get-tuple-element.44.refs_9_), channel_id=1, source_target_pairs={{0,6},{2,0},{4,2},{6,4},{1,7},{3,1},{5,3},{7,5},{8,14},{10,8},{12,... | collective-permute-start | bytes 552968 | tf_op jit(solution)/shard_map/ppermute | solution.py:421
  104.8 8.5 %collective-permute-start.14 = (bf16[144,640]{1,0:T(8,128)(2,1)S(1)}, bf16[144,640]{1,0:T(8,128)(2,1)S(1)}, u32[]{:S(2)}, u32[]{:S(2)}) collective-permute-start(bf16[144,640]{1,0:T(8,128)(2,1)S(1)} %get-tuple-element.46), channel_id=1, source_target_pairs={{0,2},{2,4},{4,6},{6,0},{1,3},{3,5},{5,7},{7,1},{8,10},{10,12},{12... | collective-permute-start | bytes 552968 | tf_op jit(solution)/shard_map/ppermute | solution.py:421
